TPU v7x, 32 devices: a whole 2x2x4 slice. The times are simulated.
32 devices in a mesh: seq: 16 (over z, y, core), fsdp: 2 (over x).
Axes of the slice: x: 2, y: 2, z: 4, core: 2. Of those that a mesh axis runs over, the one named last changes fastest.
Arguments:
- cotangent: bfloat16 [2048, 1536], P('seq', 'fsdp'), may hold values from -6 to 6
- out_weight: bfloat16 [1536, 1536], P('fsdp', 'seq'), may hold values from -0.15625 to 0.15625
- values: bfloat16 [2048, 1536], P('seq', 'fsdp'), may hold values from -1.5 to 1.5
- gate_input: bfloat16 [2048, 1536], P('seq', 'fsdp'), may hold values from -6 to 6
- conv_out: bfloat16 [2048, 1536], P('seq', 'fsdp'), may hold values from -6 to 6
- filter_taps: bfloat16 [1536, 2048], P('fsdp'), may hold values from -0.125 to 0.125
Outputs:
- grad_value: bfloat16 [2048, 1536], P('seq', 'fsdp')
- grad_gate: bfloat16 [2048, 1536], P('seq', 'fsdp')
- grad_filter: float32 [2048, 1536], P('seq', 'fsdp')
- grad_weight: float32 [1536, 1536], P('fsdp', 'seq')
All inputs are finite; a program needn't handle non-finite values.
Results may differ from a plain program's by a relative error of at most 0.007.
Values may be sent and summed in bfloat16 or wider, within the bound.
A program may use at most 128 MiB of HBM per device.

v0:
```python
import jax
import jax.numpy as jnp
from jax import lax
from jax.sharding import PartitionSpec as P


def shifted(block, axis, distance):
    devices = range(lax.axis_size(axis))
    route = [(i - distance, i) for i in devices if i - distance in devices]
    return lax.ppermute(block, axis, route)


def make_tables(block_rows):
    period = 2 * block_rows
    frequency = lax.broadcasted_iota(jnp.int32, (period, period), 0)
    position = lax.broadcasted_iota(jnp.int32, (period, period), 1)
    angles = (frequency * position % period).astype(jnp.float32) * (2.0 * jnp.pi / period)
    cosine = jnp.cos(angles)
    sine_part = jnp.sin(angles)
    parity = 1.0 - 2.0 * (position % 2).astype(jnp.float32)
    dft_cos = cosine.astype(jnp.bfloat16)
    dft_sin = (-sine_part).astype(jnp.bfloat16)
    back_cos = (parity * cosine / period).astype(jnp.bfloat16)
    back_sin = (-parity * sine_part / period).astype(jnp.bfloat16)
    return (dft_cos, dft_sin, back_cos, back_sin)


def narrow_dot(left, right):
    return jnp.dot(left, right, preferred_element_type=jnp.float32)


def product_rows(table, window):
    return lax.dot_general(
        table, window, (((1,), (1,)), ((), ())), preferred_element_type=jnp.float32
    )


def spectrum(block, cos_part, sin_part):
    return (narrow_dot(cos_part, block), narrow_dot(sin_part, block))


def value_term(conv_re, conv_im, filt_re, filt_im, back_table):
    mixed_re = conv_re * filt_re + conv_im * filt_im
    mixed_im = conv_re * filt_im - conv_im * filt_re
    stacked = jnp.concatenate(
        [mixed_re.astype(jnp.bfloat16), mixed_im.astype(jnp.bfloat16)], axis=0
    )
    return narrow_dot(back_table, stacked)


def filter_term(val_re, val_im, conv_re, conv_im, back_table):
    mixed_re = val_re * conv_re + val_im * conv_im
    mixed_im = val_re * conv_im - val_im * conv_re
    stacked = jnp.concatenate(
        [mixed_re.astype(jnp.bfloat16), mixed_im.astype(jnp.bfloat16)], axis=0
    )
    return narrow_dot(back_table, stacked)


def body(cotangent, out_weight, values, gate_input, conv_out, filter_taps):
    block_rows, channels = values.shape
    cycle_size = lax.axis_size("seq")
    weight_rows = lax.all_gather(out_weight, "seq", axis=1, tiled=True)
    features = lax.all_gather(cotangent, "fsdp", axis=1, tiled=True)
    grad_mixed = lax.dot_general(
        features, weight_rows, (((1,), (1,)), ((), ())), preferred_element_type=jnp.float32
    )
    gate_wide = gate_input.astype(jnp.float32)
    conv_wide = conv_out.astype(jnp.float32)
    grad_gate = (grad_mixed * conv_wide).astype(jnp.bfloat16)
    grad_conv = (grad_mixed * gate_wide).astype(jnp.bfloat16)
    gated = (gate_wide * conv_wide).astype(jnp.bfloat16)
    weight_terms = lax.dot_general(
        gated, features, (((0,), (0,)), ((), ())), preferred_element_type=jnp.float32
    )
    grad_weight = lax.psum_scatter(weight_terms, "seq", scatter_dimension=1, tiled=True)
    period = 2 * block_rows
    dft_cos, dft_sin, back_cos, back_sin = make_tables(block_rows)
    block_cos = dft_cos[:, :block_rows]
    block_sin = dft_sin[:, :block_rows]
    value_back = jnp.concatenate([back_cos[:block_rows], -back_sin[:block_rows]], axis=1)
    filter_back = jnp.concatenate([back_cos, back_sin], axis=1)
    padded_taps = jnp.concatenate(
        [jnp.zeros((channels, block_rows), jnp.bfloat16), filter_taps], axis=1
    )
    empty = jnp.zeros((block_rows, channels), jnp.float32)

    def window_spectrum(offset):
        window = lax.dynamic_slice_in_dim(padded_taps, offset * block_rows, period, 1)
        return (product_rows(dft_cos, window), product_rows(dft_sin, window))

    val_re, val_im = spectrum(values, block_cos, block_sin)

    def turn(offset, carry):
        incoming, grad_total, lag_grad = carry
        conv_re, conv_im = spectrum(incoming, block_cos, block_sin)
        filt_re, filt_im = window_spectrum(offset)
        grad_total = grad_total + value_term(conv_re, conv_im, filt_re, filt_im, value_back)
        start = offset * block_rows
        current = lax.dynamic_slice_in_dim(lag_grad, start, period, 0)
        update = current + filter_term(val_re, val_im, conv_re, conv_im, filter_back)
        lag_grad = lax.dynamic_update_slice_in_dim(lag_grad, update, start, 0)
        return (incoming, grad_total, lag_grad)

    def shifted_turn(offset, carry):
        incoming = shifted(carry[0], "seq", -1)
        return turn(offset, (incoming, carry[1], carry[2]))

    lag_zero = jnp.zeros(((cycle_size + 1) * block_rows, channels), jnp.float32)
    carry = turn(0, (grad_conv, empty, lag_zero))
    carry = lax.fori_loop(1, cycle_size, shifted_turn, carry)
    grad_total = carry[1]
    grad_filter = lax.psum_scatter(carry[2][block_rows:], "seq", scatter_dimension=0, tiled=True)
    return (grad_total.astype(jnp.bfloat16), grad_gate, grad_filter, grad_weight)


def solution(mesh):
    in_specs = (
        P("seq", "fsdp"),
        P("fsdp", "seq"),
        P("seq", "fsdp"),
        P("seq", "fsdp"),
        P("seq", "fsdp"),
        P("fsdp", None),
    )
    out_specs = (P("seq", "fsdp"), P("seq", "fsdp"), P("seq", "fsdp"), P("fsdp", "seq"))
    return jax.shard_map(body, mesh=mesh, in_specs=in_specs, out_specs=out_specs, check_vma=False)
```

profile of v0, /device:TPU:0, one launch (start us, length us, event | category | flops | bytes accessed | tf_op | source)
XLA Modules:
  0.0 435.8 jit_solution(12603263606972282244)
XLA Ops:
  8.0 8.8 %all_gather.6 = bf16[128,1536]{1,0:T(8,128)(2,1)S(1)} all-gather(bf16[128,768]{1,0:T(8,128)(2,1)} %param.8), channel_id=1, replica_groups=mesh['seq'=16,'fsdp'=2] {'fsdp'}, dimensions={1}, use_global_device_ids=true | all-gather | bytes 589824 | tf_op jit(solution)/shard_map/all_gather | solution.py:64
  17.5 4.0 fusion.53
  34.4 4.0 concatenate.30
  39.0 16.2 %all-gather.2.cloned.1.call-done = bf16[768,1536]{0,1:T(8,128)(2,1)} async-done(((bf16[768,96]{0,1:T(8,128)(2,1)}), bf16[768,1536]{0,1:T(8,128)(2,1)}) %all-gather.2.cloned.1.call-update) | async-done | bytes 2359312 | tf_op jit(solution)/shard_map/all_gather | solution.py:63
  55.3 2.9 fusion.41
  63.1 3.2 dynamic_update_slice.10.clone2
  66.4 251.7 %while.18 = (s32[]{:T(128)}, bf16[128,768]{1,0:T(8,128)(2,1)}, f32[128,768]{0,1:T(8,128)}, f32[2176,768]{1,0:T(8,128)}, bf16[256,128]{1,0:T(8,128)(2,1)}, /*inde...) while((s32[]{:T(128)}, bf16[128,768]{1,0:T(8,128)(2,1)}, ...), condition=%wide.region_1.2_spmd.clone, body=%wide.region_0.0_spmd.clone.sunk | while | flops 612597760 | bytes 25166124 | solution.py:111
  68.9 3.1 convolution_bitcast_fusion.6
  79.7 2.5 fusion.120
  85.3 3.1 convolution_bitcast_fusion.6
  96.0 2.4 fusion.120
  101.6 3.1 convolution_bitcast_fusion.6
  112.3 2.4 fusion.120
  118.0 3.1 convolution_bitcast_fusion.6
  128.7 2.5 fusion.120
  134.3 3.1 convolution_bitcast_fusion.6
  145.1 2.4 fusion.120
  150.7 3.1 convolution_bitcast_fusion.6
  162.0 2.4 fusion.120
  167.6 3.1 convolution_bitcast_fusion.6
  179.3 2.4 fusion.120
  185.0 3.1 convolution_bitcast_fusion.6
  201.9 3.1 convolution_bitcast_fusion.6
  218.8 3.1 convolution_bitcast_fusion.6
  230.2 2.4 fusion.120
  235.8 3.1 convolution_bitcast_fusion.6
  252.7 3.1 convolution_bitcast_fusion.6
  269.7 3.1 convolution_bitcast_fusion.6
  286.7 3.1 convolution_bitcast_fusion.6
  303.6 3.1 convolution_bitcast_fusion.6
  318.1 5.9 %slice.27 = f32[2048,768]{1,0:T(8,128)} slice(f32[2176,768]{1,0:T(8,128)} %get-tuple-element.220), slice={[128:2176], [0:768]} | slice | bytes 12582912 | tf_op jit(solution)/shard_map/slice | solution.py:113
  325.7 103.6 %reduce-scatter.3.cloned.1.call-done = f32[128,768]{1,0:T(8,128)} async-done(((f32[2048,768]{1,0:T(8,128)}), f32[128,768]{1,0:T(8,128)}) %reduce-scatter.3.cloned.1.call-update) | async-done | bytes 393232 | tf_op jit(solution)/shard_map/reduce_scatter | solution.py:113
  (291 shorter events, 206.7 us)
Async XLA Ops:
  7.2 26.1 %copy-start = (bf16[128,768]{1,0:T(8,128)(2,1)S(1)}, bf16[128,768]{1,0:T(8,128)(2,1)}, u32[]{:S(2)}) copy-start(bf16[128,768]{1,0:T(8,128)(2,1)} %param.10) | copy-start | bytes 589828
  7.2 48.1 %all-gather.2.cloned.1.call-start = ((), (), s32[]{:S(2)}) async-start(), calls=%async_computation.2 | async-start | bytes 2506752 | tf_op jit(solution)/shard_map/all_gather | solution.py:63
  7.9 317.8 %reduce-scatter.5.cloned.1.call-start = ((), (), s32[]{:S(2)}) async-start(), calls=%async_computation.4 | async-start | bytes 5013504 | tf_op jit(solution)/shard_map/reduce_scatter | solution.py:76
  21.4 5.6 %copy-start.1 = (bf16[768,2048]{1,0:T(8,128)(2,1)S(1)}, bf16[768,2048]{1,0:T(8,128)(2,1)}, u32[]{:S(2)}) copy-start(bf16[768,2048]{1,0:T(8,128)(2,1)} %param.13) | copy-start | bytes 9437188
  21.5 407.8 %reduce-scatter.3.cloned.1.call-start = ((), (), s32[]{:S(2)}) async-start(), calls=%async_computation.3 | async-start | bytes 6684672 | tf_op jit(solution)/shard_map/reduce_scatter | solution.py:113
  34.3 4.0 copy-start.16
  34.3 20.9 %copy-start.5 = (bf16[128,1536]{1,0:T(8,128)(2,1)S(1)}, bf16[128,1536]{1,0:T(8,128)(2,1)}, u32[]{:S(2)}) copy-start(bf16[128,1536]{1,0:T(8,128)(2,1)} %copy-done.4) | copy-start | bytes 1179652
  34.4 20.9 %copy-start.8 = (bf16[128,768]{1,0:T(8,128)(2,1)S(1)}, bf16[128,768]{1,0:T(8,128)(2,1)}, u32[]{:S(2)}) copy-start(bf16[128,768]{1,0:T(8,128)(2,1)} %param.12) | copy-start | bytes 589828
  34.4 20.9 %copy-start.9 = (bf16[128,768]{1,0:T(8,128)(2,1)S(1)}, bf16[128,768]{1,0:T(8,128)(2,1)}, u32[]{:S(2)}) copy-start(bf16[128,768]{1,0:T(8,128)(2,1)} %param.11) | copy-start | bytes 589828
  38.4 22.2 %copy-start.6 = (f32[256,768]{1,0:T(8,128)S(1)}, f32[256,768]{1,0:T(8,128)}, u32[]{:S(2)}) copy-start(f32[256,768]{1,0:T(8,128)} %fusion.45) | copy-start | bytes 2359300
  38.4 22.2 %copy-start.7 = (f32[256,768]{1,0:T(8,128)S(1)}, f32[256,768]{1,0:T(8,128)}, u32[]{:S(2)}) copy-start(f32[256,768]{1,0:T(8,128)} %fusion.43) | copy-start | bytes 2359300
  66.4 8.2 %collective-permute-start = (bf16[128,768]{1,0:T(8,128)(2,1)}, bf16[128,768]{1,0:T(8,128)(2,1)S(1)}, u32[]{:S(2)}, u32[]{:S(2)}) collective-permute-start(bf16[128,768]{1,0:T(8,128)(2,1)} %get-tuple-element.389), channel_id=1, source_target_pairs={{2,0},{4,2},{6,4},{8,6},{10,8},{12,10},{14,12},{16,14},{18,16},{20... | collective-permute-start | bytes 589832 | tf_op jit(solution)/shard_map/while/body/eval_jaxpr/ppermute | solution.py:10
  82.8 8.1 %collective-permute-start = (bf16[128,768]{1,0:T(8,128)(2,1)}, bf16[128,768]{1,0:T(8,128)(2,1)S(1)}, u32[]{:S(2)}, u32[]{:S(2)}) collective-permute-start(bf16[128,768]{1,0:T(8,128)(2,1)} %get-tuple-element.389), channel_id=1, source_target_pairs={{2,0},{4,2},{6,4},{8,6},{10,8},{12,10},{14,12},{16,14},{18,16},{20... | collective-permute-start | bytes 589832 | tf_op jit(solution)/shard_map/while/body/eval_jaxpr/ppermute | solution.py:10
  99.1 8.1 %collective-permute-start = (bf16[128,768]{1,0:T(8,128)(2,1)}, bf16[128,768]{1,0:T(8,128)(2,1)S(1)}, u32[]{:S(2)}, u32[]{:S(2)}) collective-permute-start(bf16[128,768]{1,0:T(8,128)(2,1)} %get-tuple-element.389), channel_id=1, source_target_pairs={{2,0},{4,2},{6,4},{8,6},{10,8},{12,10},{14,12},{16,14},{18,16},{20... | collective-permute-start | bytes 589832 | tf_op jit(solution)/shard_map/while/body/eval_jaxpr/ppermute | solution.py:10
  115.5 8.1 %collective-permute-start = (bf16[128,768]{1,0:T(8,128)(2,1)}, bf16[128,768]{1,0:T(8,128)(2,1)S(1)}, u32[]{:S(2)}, u32[]{:S(2)}) collective-permute-start(bf16[128,768]{1,0:T(8,128)(2,1)} %get-tuple-element.389), channel_id=1, source_target_pairs={{2,0},{4,2},{6,4},{8,6},{10,8},{12,10},{14,12},{16,14},{18,16},{20... | collective-permute-start | bytes 589832 | tf_op jit(solution)/shard_map/while/body/eval_jaxpr/ppermute | solution.py:10
  131.8 8.2 %collective-permute-start = (bf16[128,768]{1,0:T(8,128)(2,1)}, bf16[128,768]{1,0:T(8,128)(2,1)S(1)}, u32[]{:S(2)}, u32[]{:S(2)}) collective-permute-start(bf16[128,768]{1,0:T(8,128)(2,1)} %get-tuple-element.389), channel_id=1, source_target_pairs={{2,0},{4,2},{6,4},{8,6},{10,8},{12,10},{14,12},{16,14},{18,16},{20... | collective-permute-start | bytes 589832 | tf_op jit(solution)/shard_map/while/body/eval_jaxpr/ppermute | solution.py:10
  148.2 8.7 %collective-permute-start = (bf16[128,768]{1,0:T(8,128)(2,1)}, bf16[128,768]{1,0:T(8,128)(2,1)S(1)}, u32[]{:S(2)}, u32[]{:S(2)}) collective-permute-start(bf16[128,768]{1,0:T(8,128)(2,1)} %get-tuple-element.389), channel_id=1, source_target_pairs={{2,0},{4,2},{6,4},{8,6},{10,8},{12,10},{14,12},{16,14},{18,16},{20... | collective-permute-start | bytes 589832 | tf_op jit(solution)/shard_map/while/body/eval_jaxpr/ppermute | solution.py:10
  154.0 4.0 copy-start.2
  165.1 9.1 %collective-permute-start = (bf16[128,768]{1,0:T(8,128)(2,1)}, bf16[128,768]{1,0:T(8,128)(2,1)S(1)}, u32[]{:S(2)}, u32[]{:S(2)}) collective-permute-start(bf16[128,768]{1,0:T(8,128)(2,1)} %get-tuple-element.389), channel_id=1, source_target_pairs={{2,0},{4,2},{6,4},{8,6},{10,8},{12,10},{14,12},{16,14},{18,16},{20... | collective-permute-start | bytes 589832 | tf_op jit(solution)/shard_map/while/body/eval_jaxpr/ppermute | solution.py:10
  170.9 4.4 %copy-start.2 = (f32[256,768]{1,0:T(8,128)S(1)}, f32[256,768]{1,0:T(8,128)}, u32[]{:S(2)}) copy-start(f32[256,768]{1,0:T(8,128)} %convolution_bitcast_fusion.6) | copy-start | bytes 2359300 | tf_op jit(solution)/shard_map/while
  182.5 8.7 %collective-permute-start = (bf16[128,768]{1,0:T(8,128)(2,1)}, bf16[128,768]{1,0:T(8,128)(2,1)S(1)}, u32[]{:S(2)}, u32[]{:S(2)}) collective-permute-start(bf16[128,768]{1,0:T(8,128)(2,1)} %get-tuple-element.389), channel_id=1, source_target_pairs={{2,0},{4,2},{6,4},{8,6},{10,8},{12,10},{14,12},{16,14},{18,16},{20... | collective-permute-start | bytes 589832 | tf_op jit(solution)/shard_map/while/body/eval_jaxpr/ppermute | solution.py:10
  199.4 8.7 %collective-permute-start = (bf16[128,768]{1,0:T(8,128)(2,1)}, bf16[128,768]{1,0:T(8,128)(2,1)S(1)}, u32[]{:S(2)}, u32[]{:S(2)}) collective-permute-start(bf16[128,768]{1,0:T(8,128)(2,1)} %get-tuple-element.389), channel_id=1, source_target_pairs={{2,0},{4,2},{6,4},{8,6},{10,8},{12,10},{14,12},{16,14},{18,16},{20... | collective-permute-start | bytes 589832 | tf_op jit(solution)/shard_map/while/body/eval_jaxpr/ppermute | solution.py:10
  216.3 8.7 %collective-permute-start = (bf16[128,768]{1,0:T(8,128)(2,1)}, bf16[128,768]{1,0:T(8,128)(2,1)S(1)}, u32[]{:S(2)}, u32[]{:S(2)}) collective-permute-start(bf16[128,768]{1,0:T(8,128)(2,1)} %get-tuple-element.389), channel_id=1, source_target_pairs={{2,0},{4,2},{6,4},{8,6},{10,8},{12,10},{14,12},{16,14},{18,16},{20... | collective-permute-start | bytes 589832 | tf_op jit(solution)/shard_map/while/body/eval_jaxpr/ppermute | solution.py:10
  222.1 4.0 copy-start.2
  233.3 8.7 %collective-permute-start = (bf16[128,768]{1,0:T(8,128)(2,1)}, bf16[128,768]{1,0:T(8,128)(2,1)S(1)}, u32[]{:S(2)}, u32[]{:S(2)}) collective-permute-start(bf16[128,768]{1,0:T(8,128)(2,1)} %get-tuple-element.389), channel_id=1, source_target_pairs={{2,0},{4,2},{6,4},{8,6},{10,8},{12,10},{14,12},{16,14},{18,16},{20... | collective-permute-start | bytes 589832 | tf_op jit(solution)/shard_map/while/body/eval_jaxpr/ppermute | solution.py:10
  239.1 4.0 copy-start.2
  250.3 8.7 %collective-permute-start = (bf16[128,768]{1,0:T(8,128)(2,1)}, bf16[128,768]{1,0:T(8,128)(2,1)S(1)}, u32[]{:S(2)}, u32[]{:S(2)}) collective-permute-start(bf16[128,768]{1,0:T(8,128)(2,1)} %get-tuple-element.389), channel_id=1, source_target_pairs={{2,0},{4,2},{6,4},{8,6},{10,8},{12,10},{14,12},{16,14},{18,16},{20... | collective-permute-start | bytes 589832 | tf_op jit(solution)/shard_map/while/body/eval_jaxpr/ppermute | solution.py:10
  267.2 8.7 %collective-permute-start = (bf16[128,768]{1,0:T(8,128)(2,1)}, bf16[128,768]{1,0:T(8,128)(2,1)S(1)}, u32[]{:S(2)}, u32[]{:S(2)}) collective-permute-start(bf16[128,768]{1,0:T(8,128)(2,1)} %get-tuple-element.389), channel_id=1, source_target_pairs={{2,0},{4,2},{6,4},{8,6},{10,8},{12,10},{14,12},{16,14},{18,16},{20... | collective-permute-start | bytes 589832 | tf_op jit(solution)/shard_map/while/body/eval_jaxpr/ppermute | solution.py:10
  273.0 4.0 copy-start.2
  284.2 8.7 %collective-permute-start = (bf16[128,768]{1,0:T(8,128)(2,1)}, bf16[128,768]{1,0:T(8,128)(2,1)S(1)}, u32[]{:S(2)}, u32[]{:S(2)}) collective-permute-start(bf16[128,768]{1,0:T(8,128)(2,1)} %get-tuple-element.389), channel_id=1, source_target_pairs={{2,0},{4,2},{6,4},{8,6},{10,8},{12,10},{14,12},{16,14},{18,16},{20... | collective-permute-start | bytes 589832 | tf_op jit(solution)/shard_map/while/body/eval_jaxpr/ppermute | solution.py:10
  301.1 8.7 %collective-permute-start = (bf16[128,768]{1,0:T(8,128)(2,1)}, bf16[128,768]{1,0:T(8,128)(2,1)S(1)}, u32[]{:S(2)}, u32[]{:S(2)}) collective-permute-start(bf16[128,768]{1,0:T(8,128)(2,1)} %get-tuple-element.389), channel_id=1, source_target_pairs={{2,0},{4,2},{6,4},{8,6},{10,8},{12,10},{14,12},{16,14},{18,16},{20... | collective-permute-start | bytes 589832 | tf_op jit(solution)/shard_map/while/body/eval_jaxpr/ppermute | solution.py:10
  306.9 4.0 copy-start.2
  (32 other events, 78.7 us)
Sparse Core Ops, SparseCore 0:
  10.3 44.9 all-gather.1
  59.7 78.4 reduce-scatter.4
  324.1 105.1 reduce-scatter.2
where the time goes:
time: 440 us; the launch traced here: 436 us
  matrix products  190 us (43%)
  waiting for transfers between devices  127 us (29%)
  local copies, waits for them, and re-layouts  68.5 us (16%)
  starting transfers between devices  19.3 us (4%)
  between operations  13.9 us (3%)
  blocking collectives  8.77 us (2%)
  other arithmetic  6.08 us (1%)
    reduce_scatter x1, waiting for transfers between devices, body(): lax.psum_scatter(carry[2][block_rows:], 'seq', scatter_dimension=0, tiled...  104 us
    dot_general x66, matrix products, narrow_dot(): return jnp.dot(left, right, preferred_element_type=jnp.float32)  99.9 us
    dot_general x32, matrix products, product_rows(): lax.dot_general(table, window, (((1,), (1,)), ((), ())), preferred_elemen...  83.7 us
    dynamic_slice x30, local copies, waits for them, and re-layouts, turn(): current = lax.dynamic_slice_in_dim(lag_grad, start, period, 0)  21.8 us
    dynamic_update_slice x31, local copies, waits for them, and re-layouts, turn(): lag_grad = lax.dynamic_update_slice_in_dim(lag_grad, update, start, 0)  21.5 us
    ppermute x15, starting transfers between devices, shifted(): return lax.ppermute(block, axis, route)  19.2 us
    all_gather x1, waiting for transfers between devices, body(): weight_rows = lax.all_gather(out_weight, 'seq', axis=1, tiled=True)  16.2 us
    while x75, local copies, waits for them, and re-layouts  10.3 us
  transfers between devices with their start and end apart: 18, of which 13 were waited for; matrix products, arithmetic and copies ran while one was open for 60% of the time, Pallas kernels for 0%

commit v1 on v0

--- a/solution.py
+++ b/solution.py
@@ -1,7 +1,14 @@
+import functools
+
 import jax
 import jax.numpy as jnp
+import numpy as np
 from jax import lax
+from jax.experimental import pallas as pl
+from jax.experimental.pallas import tpu as pltpu
 from jax.sharding import PartitionSpec as P
+
+MESH = pl.DeviceIdType.MESH
 
 
 def shifted(block, axis, distance):
@@ -57,7 +64,7 @@
     return narrow_dot(back_table, stacked)
 
 
-def body(cotangent, out_weight, values, gate_input, conv_out, filter_taps):
+def ring_body(cotangent, out_weight, values, gate_input, conv_out, filter_taps):
     block_rows, channels = values.shape
     cycle_size = lax.axis_size("seq")
     weight_rows = lax.all_gather(out_weight, "seq", axis=1, tiled=True)
@@ -114,6 +121,278 @@
     return (grad_total.astype(jnp.bfloat16), grad_gate, grad_filter, grad_weight)
 
 
+def packed_tables(rows):
+    period = 2 * rows
+    freq = np.arange(rows)
+    pos = np.arange(period)
+    angle = (np.outer(pos, freq) % period) * (2.0 * np.pi / period)
+    cosine, sine = np.cos(angle), np.sin(angle)
+    alternating = 1.0 - 2.0 * (pos % 2)
+    forward_im = -sine
+    forward_im[:, 0] = alternating
+    forward = np.concatenate([cosine, forward_im], axis=1)
+    parity = (1.0 - 2.0 * (freq % 2))[:, None]
+    weight = np.where(freq == 0, 1.0, 2.0)[:, None] / period
+    back_re = weight * parity * cosine.T
+    value_im = weight * parity * sine.T
+    lag_im = -value_im
+    value_im[0] = alternating / period
+    lag_im[0] = alternating / period
+    value_back = np.concatenate([back_re, value_im], axis=0)[:, :rows]
+    lag_back = np.concatenate([back_re, lag_im], axis=0)
+    return tuple(jnp.asarray(t, jnp.bfloat16) for t in (forward, value_back, lag_back))
+
+
+def mixer_kernel(
+    n, nz,
+    cot_ref, wt_ref, val_ref, gate_ref, conv_ref, taps_ref, fwd_ref, vback_ref, lback_ref,
+    gv_ref, gg_ref, gf_ref, gw_ref,
+    feat, wall, gated_all, featq, featr, valt, valr, gct, gcr, gvt, gvr, gft, gfr,
+    taps, cre, cim, tre, tim, tmix, vre, vim, vmix, sums, lags, pw, pwr,
+    xsem, wzs, wzr, wys, wyr, wcs, wcr, gts, gtr, fts, ftr, vs, vr, cs, cr, os, orr, ls, lr, rs, rr, tsem,
+):
+    rows = cot_ref.shape[0]
+    group = gct.shape[1]
+    bf16, f32 = jnp.bfloat16, jnp.float32
+    me = lax.axis_index("seq")
+    fs = lax.axis_index("fsdp")
+    zi, q = me // 4, me % 4
+    y, core = q // 2, q % 2
+    quad = [
+        (1 - y if k >= 2 else y) * 2 + (1 - core if k % 2 else core) for k in range(4)
+    ]
+
+    def at(zshift, k):
+        return lax.rem(zi + zshift + nz, nz) * 4 + quad[k]
+
+    def send(src, dst, send_sem, recv_sem, seq, fsdp=None):
+        return pltpu.make_async_remote_copy(
+            src_ref=src, dst_ref=dst, send_sem=send_sem, recv_sem=recv_sem,
+            device_id=(seq, fs if fsdp is None else fsdp), device_id_type=MESH,
+        )
+
+    barrier = pltpu.get_barrier_semaphore()
+    for k in range(1, n):
+        pl.semaphore_signal(
+            barrier, inc=1, device_id=(lax.rem(me + k, n), fs), device_id_type=MESH
+        )
+    pl.semaphore_signal(barrier, inc=1, device_id=(me, 1 - fs), device_id_type=MESH)
+    pl.semaphore_wait(barrier, n)
+
+    pending = []
+
+    def go(copy):
+        copy.start()
+        pending.append(copy)
+        return copy
+
+    x_copy = go(send(cot_ref, feat.at[fs], xsem.at[0], xsem.at[1], me, 1 - fs))
+    for k in range(1, nz):
+        go(send(wt_ref, wall.at[me], wzs.at[k], wzr.at[k], at(k, 0)))
+    go(send(wt_ref, wall.at[me], wys.at[0], wyr.at[0], at(0, 2)))
+    go(send(wt_ref, wall.at[me], wcs.at[0], wcr.at[0], at(0, 1)))
+    taps_copy = pltpu.make_async_copy(
+        taps_ref.at[pl.ds(pl.multiple_of(me * group, group), group), :],
+        taps.at[:, rows:], tsem.at[0],
+    )
+    taps_copy.start()
+    feat[fs] = cot_ref[...]
+    wall[me] = wt_ref[...]
+    taps[:, :rows] = jnp.zeros((group, rows), bf16)
+
+    def all_to_all(src, dst, send_sems, recv_sems):
+        dst[me] = src[me]
+        for k in range(1, n):
+            to = lax.rem(me + k, n)
+            go(send(src.at[to], dst.at[me], send_sems.at[k], recv_sems.at[k], to))
+
+    def arrive(src, dst, send_sems, recv_sems):
+        for k in range(1, n):
+            origin = lax.rem(me + n - k, n)
+            send(src.at[me], dst.at[origin], send_sems.at[k], recv_sems.at[k], origin).wait_recv()
+
+    valt[...] = val_ref[...].astype(f32).T.astype(bf16).reshape(n, group, rows)
+    all_to_all(valt, valr, vs, vr)
+    gate_wide = gate_ref[...].astype(f32)
+    conv_wide = conv_ref[...].astype(f32)
+    gated_all[q] = (gate_wide * conv_wide).astype(bf16)
+    for k in range(1, 4):
+        go(send(gated_all.at[q], gated_all.at[q], gts.at[k], gtr.at[k], at(0, k)))
+
+    for k in range(1, nz):
+        slot = wall.at[at(-k, 0)]
+        send(wt_ref, slot, wzs.at[k], wzr.at[k], at(k, 0)).wait_recv()
+        go(send(slot, slot, wys.at[k], wyr.at[k], at(0, 2)))
+        go(send(slot, slot, wcs.at[k], wcr.at[k], at(0, 1)))
+
+    x_copy.wait_recv()
+    for part in range(2):
+        turned = feat[part].astype(f32).T.astype(bf16)
+        per = turned.shape[0] // n * 2
+        for j in range(n // 2):
+            s = part * (n // 2) + j
+            featq[s % 4, s // 4] = turned[j * per:(j + 1) * per]
+    featr[q] = featq[q]
+    for k in range(1, 4):
+        go(send(featq.at[quad[k]], featr.at[q], fts.at[k], ftr.at[k], at(0, k)))
+
+    for k in range(nz):
+        slot = wall.at[at(-k, 2)]
+        send(slot, slot, wys.at[k], wyr.at[k], at(0, 2)).wait_recv()
+        go(send(slot, slot, wcs.at[nz + k], wcr.at[nz + k], at(0, 1)))
+
+    lane = lax.broadcasted_iota(jnp.int32, (group, rows), 1)
+
+    def split(spec, re_ref, im_ref, mix_ref, j, sign):
+        real, imag = spec[:, :rows], spec[:, rows:]
+        re_ref[j] = real
+        if mix_ref is None:
+            im_ref[j] = imag
+        else:
+            im_ref[j] = jnp.where(lane == 0, 0.0, imag)
+            mix_ref[j] = jnp.where(lane == 0, sign * imag, real)
+
+    def spectra(source, re_ref, im_ref, mix_ref):
+        def one(j, carry):
+            spec = jnp.dot(source[j], fwd_ref[:rows, :], preferred_element_type=f32)
+            split(spec, re_ref, im_ref, mix_ref, j, 1.0)
+            return carry
+        lax.fori_loop(0, n, one, 0, unroll=4)
+
+    taps_copy.wait()
+    for m in range(n):
+        spec = jnp.dot(
+            taps[:, m * rows:(m + 2) * rows], fwd_ref[...], preferred_element_type=f32
+        )
+        split(spec, tre, tim, tmix, m, -1.0)
+    arrive(valt, valr, vs, vr)
+    spectra(valr, vre, vim, vmix)
+
+    for k in range(2 * nz):
+        slot = wall.at[at(-(k % nz), 1 if k < nz else 3)]
+        send(slot, slot, wcs.at[k], wcr.at[k], at(0, 1)).wait_recv()
+    half = n // 2
+    width = wall.shape[2]
+    mixed = jnp.dot(
+        feat[0], wall[:half].reshape(-1, width), preferred_element_type=f32
+    ) + jnp.dot(feat[1], wall[half:].reshape(-1, width), preferred_element_type=f32)
+    gg_ref[...] = (mixed * conv_ref[...].astype(f32)).astype(bf16)
+    gct[...] = (mixed * gate_ref[...].astype(f32)).T.astype(bf16).reshape(n, group, rows)
+    all_to_all(gct, gcr, cs, cr)
+
+    for k in range(1, 4):
+        send(gated_all.at[q], gated_all.at[quad[k]], gts.at[k], gtr.at[k], at(0, k)).wait_recv()
+        send(featq.at[q], featr.at[quad[k]], fts.at[k], ftr.at[k], at(0, k)).wait_recv()
+    for zz in range(nz):
+        part = jnp.dot(featr[0, zz], gated_all[0], preferred_element_type=f32)
+        for k in range(1, 4):
+            part = part + jnp.dot(featr[k, zz], gated_all[k], preferred_element_type=f32)
+        pw[zz] = part.astype(bf16)
+
+        @pl.when(zz == zi)
+        def _():
+            gw_ref[...] = part
+
+    for k in range(1, nz):
+        to = lax.rem(zi + k, nz)
+        go(send(pw.at[to], pwr.at[k - 1], rs.at[k], rr.at[k], at(k, 0)))
+
+    arrive(gct, gcr, cs, cr)
+    spectra(gcr, cre, cim, None)
+
+    def value_rows(r, carry):
+        at_rows = pl.ds(pl.multiple_of(r * 8, 8), 8)
+        for i in range(n):
+            c_re, c_im = cre[i:n, at_rows, :], cim[i:n, at_rows, :]
+            t_re, t_im = tre[:n - i, at_rows, :], tim[:n - i, at_rows, :]
+            t_mix = tmix[:n - i, at_rows, :]
+            sums[i, at_rows, :rows] = jnp.sum(c_re * t_re + c_im * t_im, axis=0)
+            sums[i, at_rows, rows:] = jnp.sum(c_re * t_im - c_im * t_mix, axis=0)
+        return carry
+
+    lax.fori_loop(0, group // 8, value_rows, 0)
+    packed = sums[...].astype(bf16).reshape(n * group, 2 * rows)
+    blocks = jnp.dot(packed, vback_ref[...], preferred_element_type=f32)
+    gvt[...] = blocks.astype(bf16).reshape(n, group, rows)
+    all_to_all(gvt, gvr, os, orr)
+
+    def lag_rows(r, carry):
+        at_rows = pl.ds(pl.multiple_of(r * 8, 8), 8)
+        for m in range(n):
+            c_re, c_im = cre[m:n, at_rows, :], cim[m:n, at_rows, :]
+            v_re, v_im = vre[:n - m, at_rows, :], vim[:n - m, at_rows, :]
+            v_mix = vmix[:n - m, at_rows, :]
+            lags[m, at_rows, :rows] = jnp.sum(v_re * c_re + v_im * c_im, axis=0)
+            lags[m, at_rows, rows:] = jnp.sum(v_mix * c_im - v_im * c_re, axis=0)
+        return carry
+
+    lax.fori_loop(0, group // 8, lag_rows, 0)
+    packed = lags[...].astype(bf16).reshape(n * group, 2 * rows)
+    parts = jnp.dot(packed, lback_ref[...], preferred_element_type=f32)
+    first = jnp.concatenate([parts[group:, :rows], jnp.zeros((group, rows), f32)], axis=0)
+    gft[...] = (parts[:, rows:] + first).astype(bf16).reshape(n, group, rows)
+    all_to_all(gft, gfr, ls, lr)
+
+    for k in range(1, nz):
+        send(pw.at[0], pwr.at[k - 1], rs.at[k], rr.at[k], at(k, 0)).wait_recv()
+        gw_ref[...] += pwr[k - 1].astype(f32)
+    arrive(gvt, gvr, os, orr)
+    gv_ref[...] = gvr[...].reshape(n * group, rows)
+    arrive(gft, gfr, ls, lr)
+    gf_ref[...] = gfr[...].reshape(n * group, rows).astype(f32)
+    for copy in pending:
+        copy.wait_send()
+
+
+def split_body(cotangent, out_weight, values, gate_input, conv_out, filter_taps):
+    rows, channels = values.shape
+    n = lax.axis_size("seq")
+    nz = n // 4
+    group = channels // n
+    slice_cols = out_weight.shape[1]
+    forward, value_back, lag_back = packed_tables(rows)
+    bf16, f32 = jnp.bfloat16, jnp.float32
+    vm = pltpu.VMEM
+    dma = pltpu.SemaphoreType.DMA
+    trip = (n, group, rows)
+    vmem = pl.BlockSpec(memory_space=pltpu.VMEM)
+    gv, gg, gf, gw = pl.pallas_call(
+        functools.partial(mixer_kernel, n, nz),
+        out_shape=(
+            jax.ShapeDtypeStruct((channels, rows), bf16),
+            jax.ShapeDtypeStruct((rows, channels), bf16),
+            jax.ShapeDtypeStruct((channels, rows), f32),
+            jax.ShapeDtypeStruct((slice_cols, channels), f32),
+        ),
+        in_specs=[vmem] * 5 + [pl.BlockSpec(memory_space=pl.ANY)] + [vmem] * 3,
+        out_specs=(vmem,) * 4,
+        scratch_shapes=[
+            vm((2, rows, channels), bf16),
+            vm((n, slice_cols, channels), bf16),
+            vm((4, rows, channels), bf16),
+            vm((4, nz, slice_cols, rows), bf16),
+            vm((4, nz, slice_cols, rows), bf16),
+        ] + [vm(trip, bf16)] * 8 + [
+            vm((group, (n + 1) * rows), bf16),
+        ] + [vm(trip, f32)] * 8 + [
+            vm((n, group, 2 * rows), f32),
+            vm((n, group, 2 * rows), f32),
+            vm((nz, slice_cols, channels), bf16),
+            vm((nz - 1, slice_cols, channels), bf16),
+            dma((2,)),
+            dma((nz,)), dma((nz,)), dma((nz,)), dma((nz,)), dma((2 * nz,)), dma((2 * nz,)),
+            dma((4,)), dma((4,)), dma((4,)), dma((4,)),
+        ] + [dma((n,))] * 8 + [dma((nz,)), dma((nz,)), dma((1,))],
+        compiler_params=pltpu.CompilerParams(
+            collective_id=0, has_side_effects=True, vmem_limit_bytes=48 * 1024 * 1024
+        ),
+    )(
+        cotangent, out_weight.T, values, gate_input, conv_out, filter_taps,
+        forward, value_back, lag_back,
+    )
+    return gv.T, gg, gf.T, gw.T
+
+
 def solution(mesh):
     in_specs = (
         P("seq", "fsdp"),
@@ -124,4 +403,13 @@
         P("fsdp", None),
     )
     out_specs = (P("seq", "fsdp"), P("seq", "fsdp"), P("seq", "fsdp"), P("fsdp", "seq"))
+
+    def body(*blocks):
+        rows, channels = blocks[2].shape
+        n = mesh.shape["seq"]
+        aligned = rows % 128 == 0 and channels % (16 * n) == 0 and blocks[1].shape[1] % 16 == 0
+        if aligned and n % 8 == 0 and mesh.shape["fsdp"] == 2:
+            return split_body(*blocks)
+        return ring_body(*blocks)
+
     return jax.shard_map(body, mesh=mesh, in_specs=in_specs, out_specs=out_specs, check_vma=False)

time: 440 us -> 74.2 us (0.17)
  matrix products: 190 us -> 0 us
  waiting for transfers between devices: 127 us -> 0 us
  Pallas kernels: 0 us -> 60.9 us
  local copies, waits for them, and re-layouts: 68.5 us -> 12.3 us
  starting transfers between devices: 19.3 us -> 0 us
  between operations: 13.9 us -> 0.66 us
  blocking collectives: 8.77 us -> 0 us
  other arithmetic: 6.08 us -> 0 us
    dot_general x100 -> x0, matrix products: 190 us -> none  [the longest x66 99.9 us: narrow_dot(): return jnp.dot(left, right, preferred_element_type=jnp.float32)]
    reduce_scatter x2 -> x0, waiting for transfers between devices: 104 us -> none  [the longest x1 104 us: body(): lax.psum_scatter(carry[2][block_rows:], 'seq', scatter_dimension=0, tiled...]
    pallas_call x0 -> x1, Pallas kernels: none -> 60.9 us  [split_body(): pl.pallas_call(functools.partial(mixer_kernel, n, nz), out_shape=(jax.Sha...]
    dynamic_slice x30 -> x0, local copies, waits for them, and re-layouts: 21.8 us -> none  [turn(): current = lax.dynamic_slice_in_dim(lag_grad, start, period, 0)]
    dynamic_update_slice x31 -> x0, local copies, waits for them, and re-layouts: 21.5 us -> none  [turn(): lag_grad = lax.dynamic_update_slice_in_dim(lag_grad, update, start, 0)]
    ppermute x15 -> x0, starting transfers between devices: 19.2 us -> none  [shifted(): return lax.ppermute(block, axis, route)]
    all_gather x1 -> x0, waiting for transfers between devices: 16.2 us -> none  [body(): weight_rows = lax.all_gather(out_weight, 'seq', axis=1, tiled=True)]
    while x76 -> x0, local copies, waits for them, and re-layouts: 11.1 us -> none
  transfers between devices with their start and end apart: 18 -> 0, of which waited for: 13 -> 0; matrix products, arithmetic and copies ran while one was open for 60% -> 0% of each run, Pallas kernels for 0% -> 0%
where the time goes in v1:
time: 74.2 us; the launch traced here: 73.9 us
  Pallas kernels  60.9 us (82%)
  local copies, waits for them, and re-layouts  12.3 us (17%)
    pallas_call x1, Pallas kernels, split_body(): pl.pallas_call(functools.partial(mixer_kernel, n, nz), out_shape=(jax.Sha...  60.9 us
    unnamed x22, local copies, waits for them, and re-layouts  12.3 us

profile of v1, /device:TPU:0, one launch (start us, length us, event | category | flops | bytes accessed | tf_op | source)
XLA Modules:
  0.0 73.9 jit_solution(13724455315361948476)
XLA Ops:
  0.6 0.0 copy-start
  0.6 1.9 %copy-done = bf16[768,2048]{1,0:T(8,128)(2,1)S(1)} copy-done((bf16[768,2048]{1,0:T(8,128)(2,1)S(1)}, bf16[768,2048]{1,0:T(8,128)(2,1)}, u32[]{:S(2)}) %copy-start) | copy-done | bytes 3145752
  2.5 0.0 copy-start.1
  2.5 0.9 %copy-done.1 = bf16[128,768]{1,0:T(8,128)(2,1)S(1)} copy-done((bf16[128,768]{1,0:T(8,128)(2,1)S(1)}, bf16[128,768]{1,0:T(8,128)(2,1)}, u32[]{:S(2)}) %copy-start.1) | copy-done | bytes 196632
  3.5 0.0 copy-start.2
  3.5 0.9 %copy-done.2 = bf16[128,768]{1,0:T(8,128)(2,1)S(1)} copy-done((bf16[128,768]{1,0:T(8,128)(2,1)S(1)}, bf16[128,768]{1,0:T(8,128)(2,1)}, u32[]{:S(2)}) %copy-start.2) | copy-done | bytes 196632
  4.4 0.0 copy-start.3
  4.4 0.9 %copy-done.3 = bf16[128,768]{1,0:T(8,128)(2,1)S(1)} copy-done((bf16[128,768]{1,0:T(8,128)(2,1)S(1)}, bf16[128,768]{1,0:T(8,128)(2,1)}, u32[]{:S(2)}) %copy-start.3) | copy-done | bytes 196632
  5.3 0.0 copy-start.4
  5.3 0.9 %copy-done.4 = bf16[128,768]{1,0:T(8,128)(2,1)S(1)} copy-done((bf16[128,768]{1,0:T(8,128)(2,1)S(1)}, bf16[128,768]{1,0:T(8,128)(2,1)}, u32[]{:S(2)}) %copy-start.4) | copy-done | bytes 196632
  6.2 0.0 copy-start.5
  6.2 0.9 %copy-done.5 = bf16[768,96]{0,1:T(8,128)(2,1)S(1)} copy-done((bf16[768,96]{0,1:T(8,128)(2,1)S(1)}, bf16[768,96]{0,1:T(8,128)(2,1)}, u32[]{:S(2)}) %copy-start.5) | copy-done | bytes 147480
  7.1 0.0 copy-start.6
  7.1 0.9 %copy-done.6 = bf16[256,256]{1,0:T(8,128)(2,1)S(1)} copy-done((bf16[256,256]{1,0:T(8,128)(2,1)S(1)}, bf16[256,256]{1,0:T(8,128)(2,1)}, u32[]{:S(2)}) %copy-start.6) | copy-done | bytes 131096
  8.0 0.0 copy-start.7
  8.1 0.9 %copy-done.7 = bf16[256,256]{1,0:T(8,128)(2,1)S(1)} copy-done((bf16[256,256]{1,0:T(8,128)(2,1)S(1)}, bf16[256,256]{1,0:T(8,128)(2,1)}, u32[]{:S(2)}) %copy-start.7) | copy-done | bytes 131096
  9.0 0.0 copy-start.8
  9.0 0.8 %copy-done.8 = bf16[256,128]{1,0:T(8,128)(2,1)S(1)} copy-done((bf16[256,128]{1,0:T(8,128)(2,1)S(1)}, bf16[256,128]{1,0:T(8,128)(2,1)}, u32[]{:S(2)}) %copy-start.8) | copy-done | bytes 65560
  9.8 60.9 %shard_map.120 = (bf16[768,128]{1,0:T(8,128)(2,1)S(1)}, bf16[128,768]{1,0:T(8,128)(2,1)S(1)}, f32[768,128]{1,0:T(8,128)S(1)}, f32[96,768]{1,0:T(8,128)S(1)}) custom-call(bf16[128,768]{1,0:T(8,128)(2,1)S(1)} %copy-done.1, bf16[96,768]{1,0:T(8,128)(2,1)S(1)} %bitcast.7, bf16[128,768]{1,0:T(8,128)(2,1)S(1)} %copy-done.2, bf16[128,768]{1,0:T(8,128)(2,1)S(1)} %copy-done.3, ...), custom_call_target="tpu_custom_call" | custom-call | tf_op jit(solution)/shard_map/pallas_call | solution.py:359
  70.7 0.8 %copy.13 = bf16[128,768]{1,0:T(8,128)(2,1)} copy(bf16[128,768]{0,1:T(8,128)(2,1)S(1)} %bitcast.6) | data formatting | bytes 393216
  71.6 0.9 %copy.14 = f32[128,768]{1,0:T(8,128)} copy(f32[128,768]{0,1:T(8,128)S(1)} %bitcast.4) | data formatting | bytes 786432
  72.5 0.7 copy.17
  73.2 0.7 copy.18
Async XLA Ops:
  0.6 1.9 %copy-start = (bf16[768,2048]{1,0:T(8,128)(2,1)S(1)}, bf16[768,2048]{1,0:T(8,128)(2,1)}, u32[]{:S(2)}) copy-start(bf16[768,2048]{1,0:T(8,128)(2,1)} %taps_ref.1) | copy-start | bytes 9437188
  2.5 0.9 %copy-start.1 = (bf16[128,768]{1,0:T(8,128)(2,1)S(1)}, bf16[128,768]{1,0:T(8,128)(2,1)}, u32[]{:S(2)}) copy-start(bf16[128,768]{1,0:T(8,128)(2,1)} %cot_ref.1) | copy-start | bytes 589828
  3.5 0.9 %copy-start.2 = (bf16[128,768]{1,0:T(8,128)(2,1)S(1)}, bf16[128,768]{1,0:T(8,128)(2,1)}, u32[]{:S(2)}) copy-start(bf16[128,768]{1,0:T(8,128)(2,1)} %val_ref.1) | copy-start | bytes 589828
  4.4 0.9 %copy-start.3 = (bf16[128,768]{1,0:T(8,128)(2,1)S(1)}, bf16[128,768]{1,0:T(8,128)(2,1)}, u32[]{:S(2)}) copy-start(bf16[128,768]{1,0:T(8,128)(2,1)} %gate_ref.1) | copy-start | bytes 589828
  5.3 0.9 %copy-start.4 = (bf16[128,768]{1,0:T(8,128)(2,1)S(1)}, bf16[128,768]{1,0:T(8,128)(2,1)}, u32[]{:S(2)}) copy-start(bf16[128,768]{1,0:T(8,128)(2,1)} %conv_ref.1) | copy-start | bytes 589828
  6.2 0.9 %copy-start.5 = (bf16[768,96]{0,1:T(8,128)(2,1)S(1)}, bf16[768,96]{0,1:T(8,128)(2,1)}, u32[]{:S(2)}) copy-start(bf16[768,96]{0,1:T(8,128)(2,1)} %param.10) | copy-start | bytes 442372
  7.1 0.9 %copy-start.6 = (bf16[256,256]{1,0:T(8,128)(2,1)S(1)}, bf16[256,256]{1,0:T(8,128)(2,1)}, u32[]{:S(2)}) copy-start(bf16[256,256]{1,0:T(8,128)(2,1)} %constant.8.clone.lback_ref) | copy-start | bytes 393220
  8.0 0.9 %copy-start.7 = (bf16[256,256]{1,0:T(8,128)(2,1)S(1)}, bf16[256,256]{1,0:T(8,128)(2,1)}, u32[]{:S(2)}) copy-start(bf16[256,256]{1,0:T(8,128)(2,1)} %constant.6.clone.fwd_ref) | copy-start | bytes 393220
  9.0 0.8 %copy-start.8 = (bf16[256,128]{1,0:T(8,128)(2,1)S(1)}, bf16[256,128]{1,0:T(8,128)(2,1)}, u32[]{:S(2)}) copy-start(bf16[256,128]{1,0:T(8,128)(2,1)} %constant.7.clone.vback_ref) | copy-start | bytes 196612

commit v2 on v1

--- a/solution.py
+++ b/solution.py
@@ -145,13 +145,14 @@
 
 def mixer_kernel(
     n, nz,
-    cot_ref, wt_ref, val_ref, gate_ref, conv_ref, taps_ref, fwd_ref, vback_ref, lback_ref,
+    cot_ref, wt_ref, val_ref, gate_ref, conv_ref, taps_ref, fwd_hbm, vback_hbm, lback_hbm,
     gv_ref, gg_ref, gf_ref, gw_ref,
+    val_in, gate_in, conv_in, fwd_ref, vback_ref, lback_ref,
     feat, wall, gated_all, featq, featr, valt, valr, gct, gcr, gvt, gvr, gft, gfr,
-    taps, cre, cim, tre, tim, tmix, vre, vim, vmix, sums, lags, pw, pwr,
+    taps, cre, cim, tre, tim, tmix, vre, vim, vmix, sums, lags, pw, pair_out, pair_in, cross_out, cross_in,
     xsem, wzs, wzr, wys, wyr, wcs, wcr, gts, gtr, fts, ftr, vs, vr, cs, cr, os, orr, ls, lr, rs, rr, tsem,
 ):
-    rows = cot_ref.shape[0]
+    rows = val_in.shape[0]
     group = gct.shape[1]
     bf16, f32 = jnp.bfloat16, jnp.float32
     me = lax.axis_index("seq")
@@ -161,15 +162,35 @@
     quad = [
         (1 - y if k >= 2 else y) * 2 + (1 - core if k % 2 else core) for k in range(4)
     ]
-
-    def at(zshift, k):
-        return lax.rem(zi + zshift + nz, nz) * 4 + quad[k]
+    pair = zi + 1 - 2 * (zi % 2)
+    cross = lax.rem(zi + 2, 4)
+    far = lax.rem(pair + 2, 4)
+    levels = [zi, cross, pair, far]
+
+    def at(level, k):
+        return levels[level] * 4 + quad[k]
 
     def send(src, dst, send_sem, recv_sem, seq, fsdp=None):
         return pltpu.make_async_remote_copy(
             src_ref=src, dst_ref=dst, send_sem=send_sem, recv_sem=recv_sem,
             device_id=(seq, fs if fsdp is None else fsdp), device_id_type=MESH,
         )
+
+    local = [
+        pltpu.make_async_copy(src, dst, tsem.at[i]) for i, (src, dst) in enumerate([
+            (wt_ref, wall.at[me]),
+            (cot_ref, feat.at[fs]),
+            (gate_ref, gate_in),
+            (conv_ref, conv_in),
+            (val_ref, val_in),
+            (taps_ref.at[pl.ds(pl.multiple_of(me * group, group), group), :], taps.at[:, rows:]),
+            (fwd_hbm, fwd_ref),
+            (vback_hbm, vback_ref),
+            (lback_hbm, lback_ref),
+        ])
+    ]
+    for copy in local:
+        copy.start()
 
     barrier = pltpu.get_barrier_semaphore()
     for k in range(1, n):
@@ -177,6 +198,7 @@
             barrier, inc=1, device_id=(lax.rem(me + k, n), fs), device_id_type=MESH
         )
     pl.semaphore_signal(barrier, inc=1, device_id=(me, 1 - fs), device_id_type=MESH)
+    taps[:, :rows] = jnp.zeros((group, rows), bf16)
     pl.semaphore_wait(barrier, n)
 
     pending = []
@@ -186,19 +208,12 @@
         pending.append(copy)
         return copy
 
+    own = wall.at[me]
+    go(send(wt_ref, own, wzs.at[1], wzr.at[1], at(1, 0)))
+    go(send(wt_ref, own, wzs.at[2], wzr.at[2], at(2, 0)))
+    go(send(wt_ref, own, wys.at[0], wyr.at[0], at(0, 2)))
     x_copy = go(send(cot_ref, feat.at[fs], xsem.at[0], xsem.at[1], me, 1 - fs))
-    for k in range(1, nz):
-        go(send(wt_ref, wall.at[me], wzs.at[k], wzr.at[k], at(k, 0)))
-    go(send(wt_ref, wall.at[me], wys.at[0], wyr.at[0], at(0, 2)))
-    go(send(wt_ref, wall.at[me], wcs.at[0], wcr.at[0], at(0, 1)))
-    taps_copy = pltpu.make_async_copy(
-        taps_ref.at[pl.ds(pl.multiple_of(me * group, group), group), :],
-        taps.at[:, rows:], tsem.at[0],
-    )
-    taps_copy.start()
-    feat[fs] = cot_ref[...]
-    wall[me] = wt_ref[...]
-    taps[:, :rows] = jnp.zeros((group, rows), bf16)
+    go(send(wt_ref, own, wcs.at[0], wcr.at[0], at(0, 1)))
 
     def all_to_all(src, dst, send_sems, recv_sems):
         dst[me] = src[me]
@@ -211,19 +226,50 @@
             origin = lax.rem(me + n - k, n)
             send(src.at[me], dst.at[origin], send_sems.at[k], recv_sems.at[k], origin).wait_recv()
 
-    valt[...] = val_ref[...].astype(f32).T.astype(bf16).reshape(n, group, rows)
+    for copy in local:
+        copy.wait()
+    gated_all[q] = (gate_in[...].astype(f32) * conv_in[...].astype(f32)).astype(bf16)
+    go(send(gated_all.at[q], gated_all.at[q], gts.at[1], gtr.at[1], at(0, 1)))
+    valt[...] = val_in[...].astype(f32).T.astype(bf16).reshape(n, group, rows)
+
+    def weight_from(level):
+        slot = wall.at[at(level, 0)]
+        send(slot, slot, wzs.at[level], wzr.at[level], at(level, 0)).wait_recv()
+        if level == 1:
+            go(send(slot, slot, wzs.at[3], wzr.at[3], at(2, 0)))
+        go(send(slot, slot, wys.at[level], wyr.at[level], at(0, 2)))
+        go(send(slot, slot, wcs.at[level], wcr.at[level], at(0, 1)))
+
+    weight_from(1)
+    weight_from(2)
+
+    lane = lax.broadcasted_iota(jnp.int32, (group, rows), 1)
+
+    def split(spec, re_ref, im_ref, mix_ref, j, sign):
+        real, imag = spec[:, :rows], spec[:, rows:]
+        re_ref[j] = real
+        if mix_ref is None:
+            im_ref[j] = imag
+        else:
+            im_ref[j] = jnp.where(lane == 0, 0.0, imag)
+            mix_ref[j] = jnp.where(lane == 0, sign * imag, real)
+
+    def spectra(source, re_ref, im_ref, mix_ref):
+        def one(j, carry):
+            spec = jnp.dot(source[j], fwd_ref[:rows, :], preferred_element_type=f32)
+            split(spec, re_ref, im_ref, mix_ref, j, 1.0)
+            return carry
+        lax.fori_loop(0, n, one, 0, unroll=4)
+
+    for m in range(n):
+        spec = jnp.dot(
+            taps[:, m * rows:(m + 2) * rows], fwd_ref[...], preferred_element_type=f32
+        )
+        split(spec, tre, tim, tmix, m, -1.0)
+
+    weight_from(3)
     all_to_all(valt, valr, vs, vr)
-    gate_wide = gate_ref[...].astype(f32)
-    conv_wide = conv_ref[...].astype(f32)
-    gated_all[q] = (gate_wide * conv_wide).astype(bf16)
-    for k in range(1, 4):
-        go(send(gated_all.at[q], gated_all.at[q], gts.at[k], gtr.at[k], at(0, k)))
-
-    for k in range(1, nz):
-        slot = wall.at[at(-k, 0)]
-        send(wt_ref, slot, wzs.at[k], wzr.at[k], at(k, 0)).wait_recv()
-        go(send(slot, slot, wys.at[k], wyr.at[k], at(0, 2)))
-        go(send(slot, slot, wcs.at[k], wcr.at[k], at(0, 1)))
+    go(send(gated_all.at[q], gated_all.at[q], gts.at[2], gtr.at[2], at(0, 2)))
 
     x_copy.wait_recv()
     for part in range(2):
@@ -236,67 +282,48 @@
     for k in range(1, 4):
         go(send(featq.at[quad[k]], featr.at[q], fts.at[k], ftr.at[k], at(0, k)))
 
-    for k in range(nz):
-        slot = wall.at[at(-k, 2)]
-        send(slot, slot, wys.at[k], wyr.at[k], at(0, 2)).wait_recv()
-        go(send(slot, slot, wcs.at[nz + k], wcr.at[nz + k], at(0, 1)))
-
-    lane = lax.broadcasted_iota(jnp.int32, (group, rows), 1)
-
-    def split(spec, re_ref, im_ref, mix_ref, j, sign):
-        real, imag = spec[:, :rows], spec[:, rows:]
-        re_ref[j] = real
-        if mix_ref is None:
-            im_ref[j] = imag
-        else:
-            im_ref[j] = jnp.where(lane == 0, 0.0, imag)
-            mix_ref[j] = jnp.where(lane == 0, sign * imag, real)
-
-    def spectra(source, re_ref, im_ref, mix_ref):
-        def one(j, carry):
-            spec = jnp.dot(source[j], fwd_ref[:rows, :], preferred_element_type=f32)
-            split(spec, re_ref, im_ref, mix_ref, j, 1.0)
-            return carry
-        lax.fori_loop(0, n, one, 0, unroll=4)
-
-    taps_copy.wait()
-    for m in range(n):
-        spec = jnp.dot(
-            taps[:, m * rows:(m + 2) * rows], fwd_ref[...], preferred_element_type=f32
-        )
-        split(spec, tre, tim, tmix, m, -1.0)
-    arrive(valt, valr, vs, vr)
-    spectra(valr, vre, vim, vmix)
-
+    for level in range(nz):
+        slot = wall.at[at(level, 2)]
+        send(slot, slot, wys.at[level], wyr.at[level], at(0, 2)).wait_recv()
+        go(send(slot, slot, wcs.at[nz + level], wcr.at[nz + level], at(0, 1)))
+    far_gated = gated_all.at[quad[2]]
+    send(far_gated, far_gated, gts.at[2], gtr.at[2], at(0, 2)).wait_recv()
+    go(send(far_gated, far_gated, gts.at[3], gtr.at[3], at(0, 1)))
     for k in range(2 * nz):
-        slot = wall.at[at(-(k % nz), 1 if k < nz else 3)]
+        slot = wall.at[at(k % nz, 1 if k < nz else 3)]
         send(slot, slot, wcs.at[k], wcr.at[k], at(0, 1)).wait_recv()
+
     half = n // 2
     width = wall.shape[2]
     mixed = jnp.dot(
         feat[0], wall[:half].reshape(-1, width), preferred_element_type=f32
     ) + jnp.dot(feat[1], wall[half:].reshape(-1, width), preferred_element_type=f32)
-    gg_ref[...] = (mixed * conv_ref[...].astype(f32)).astype(bf16)
-    gct[...] = (mixed * gate_ref[...].astype(f32)).T.astype(bf16).reshape(n, group, rows)
+    gct[...] = (mixed * gate_in[...].astype(f32)).T.astype(bf16).reshape(n, group, rows)
     all_to_all(gct, gcr, cs, cr)
+    gg_ref[...] = (mixed * conv_in[...].astype(f32)).astype(bf16)
 
     for k in range(1, 4):
-        send(gated_all.at[q], gated_all.at[quad[k]], gts.at[k], gtr.at[k], at(0, k)).wait_recv()
+        there = gated_all.at[quad[k]]
+        if k != 2:
+            send(there, there, gts.at[k], gtr.at[k], at(0, k)).wait_recv()
         send(featq.at[q], featr.at[quad[k]], fts.at[k], ftr.at[k], at(0, k)).wait_recv()
-    for zz in range(nz):
-        part = jnp.dot(featr[0, zz], gated_all[0], preferred_element_type=f32)
+
+    def weight_part(level):
+        z = levels[level]
+        total = jnp.dot(featr[0, z], gated_all[0], preferred_element_type=f32)
         for k in range(1, 4):
-            part = part + jnp.dot(featr[k, zz], gated_all[k], preferred_element_type=f32)
-        pw[zz] = part.astype(bf16)
-
-        @pl.when(zz == zi)
-        def _():
-            gw_ref[...] = part
-
-    for k in range(1, nz):
-        to = lax.rem(zi + k, nz)
-        go(send(pw.at[to], pwr.at[k - 1], rs.at[k], rr.at[k], at(k, 0)))
-
+            total = total + jnp.dot(featr[k, z], gated_all[k], preferred_element_type=f32)
+        return total
+
+    pair_out[0] = weight_part(3).astype(bf16)
+    go(send(pair_out.at[0], pair_in.at[0], rs.at[0], rr.at[0], at(2, 0)))
+    pair_out[1] = weight_part(2).astype(bf16)
+    go(send(pair_out.at[1], pair_in.at[1], rs.at[1], rr.at[1], at(2, 0)))
+    pw[0] = weight_part(1)
+    pw[1] = weight_part(0)
+
+    arrive(valt, valr, vs, vr)
+    spectra(valr, vre, vim, vmix)
     arrive(gct, gcr, cs, cr)
     spectra(gcr, cre, cim, None)
 
@@ -316,6 +343,10 @@
     gvt[...] = blocks.astype(bf16).reshape(n, group, rows)
     all_to_all(gvt, gvr, os, orr)
 
+    send(pair_out.at[0], pair_in.at[0], rs.at[0], rr.at[0], at(2, 0)).wait_recv()
+    cross_out[...] = (pw[0] + pair_in[0].astype(f32)).astype(bf16)
+    go(send(cross_out, cross_in, rs.at[2], rr.at[2], at(1, 0)))
+
     def lag_rows(r, carry):
         at_rows = pl.ds(pl.multiple_of(r * 8, 8), 8)
         for m in range(n):
@@ -333,9 +364,9 @@
     gft[...] = (parts[:, rows:] + first).astype(bf16).reshape(n, group, rows)
     all_to_all(gft, gfr, ls, lr)
 
-    for k in range(1, nz):
-        send(pw.at[0], pwr.at[k - 1], rs.at[k], rr.at[k], at(k, 0)).wait_recv()
-        gw_ref[...] += pwr[k - 1].astype(f32)
+    send(pair_out.at[1], pair_in.at[1], rs.at[1], rr.at[1], at(2, 0)).wait_recv()
+    send(cross_out, cross_in, rs.at[2], rr.at[2], at(1, 0)).wait_recv()
+    gw_ref[...] = pw[1] + pair_in[1].astype(f32) + cross_in[...].astype(f32)
     arrive(gvt, gvr, os, orr)
     gv_ref[...] = gvr[...].reshape(n * group, rows)
     arrive(gft, gfr, ls, lr)
@@ -364,9 +395,12 @@
             jax.ShapeDtypeStruct((channels, rows), f32),
             jax.ShapeDtypeStruct((slice_cols, channels), f32),
         ),
-        in_specs=[vmem] * 5 + [pl.BlockSpec(memory_space=pl.ANY)] + [vmem] * 3,
+        in_specs=[pl.BlockSpec(memory_space=pltpu.HBM)] * 9,
         out_specs=(vmem,) * 4,
-        scratch_shapes=[
+        scratch_shapes=[vm((rows, channels), bf16)] * 3 + [
+            vm((2 * rows, 2 * rows), bf16),
+            vm((2 * rows, rows), bf16),
+            vm((2 * rows, 2 * rows), bf16),
             vm((2, rows, channels), bf16),
             vm((n, slice_cols, channels), bf16),
             vm((4, rows, channels), bf16),
@@ -377,12 +411,15 @@
         ] + [vm(trip, f32)] * 8 + [
             vm((n, group, 2 * rows), f32),
             vm((n, group, 2 * rows), f32),
-            vm((nz, slice_cols, channels), bf16),
-            vm((nz - 1, slice_cols, channels), bf16),
+            vm((2, slice_cols, channels), f32),
+            vm((2, slice_cols, channels), bf16),
+            vm((2, slice_cols, channels), bf16),
+            vm((slice_cols, channels), bf16),
+            vm((slice_cols, channels), bf16),
             dma((2,)),
             dma((nz,)), dma((nz,)), dma((nz,)), dma((nz,)), dma((2 * nz,)), dma((2 * nz,)),
             dma((4,)), dma((4,)), dma((4,)), dma((4,)),
-        ] + [dma((n,))] * 8 + [dma((nz,)), dma((nz,)), dma((1,))],
+        ] + [dma((n,))] * 8 + [dma((3,)), dma((3,)), dma((9,))],
         compiler_params=pltpu.CompilerParams(
             collective_id=0, has_side_effects=True, vmem_limit_bytes=48 * 1024 * 1024
         ),
@@ -408,7 +445,7 @@
         rows, channels = blocks[2].shape
         n = mesh.shape["seq"]
         aligned = rows % 128 == 0 and channels % (16 * n) == 0 and blocks[1].shape[1] % 16 == 0
-        if aligned and n % 8 == 0 and mesh.shape["fsdp"] == 2:
+        if aligned and n == 16 and mesh.shape["fsdp"] == 2:
             return split_body(*blocks)
         return ring_body(*blocks)
 

time: 74.2 us -> 73.5 us (level)
  no operation moved by 1% of the time
where the time goes in v2:
time: 73.5 us; the launch traced here: 73.1 us
  Pallas kernels  60.2 us (82%)
  local copies, waits for them, and re-layouts  12.3 us (17%)
    pallas_call x1, Pallas kernels, split_body(): pl.pallas_call(functools.partial(mixer_kernel, n, nz), out_shape=(jax.Sha...  60.2 us
    unnamed x22, local copies, waits for them, and re-layouts  12.3 us

profile of v2, /device:TPU:0, one launch (start us, length us, event | category | flops | bytes accessed | tf_op | source)
XLA Modules:
  0.0 73.1 jit_solution(7398244274491480448)
XLA Ops:
  0.6 0.0 copy-start
  0.6 1.9 %copy-done = bf16[768,2048]{1,0:T(8,128)(2,1)S(1)} copy-done((bf16[768,2048]{1,0:T(8,128)(2,1)S(1)}, bf16[768,2048]{1,0:T(8,128)(2,1)}, u32[]{:S(2)}) %copy-start) | copy-done | bytes 3145752
  2.5 0.0 copy-start.1
  2.5 0.9 %copy-done.1 = bf16[128,768]{1,0:T(8,128)(2,1)S(1)} copy-done((bf16[128,768]{1,0:T(8,128)(2,1)S(1)}, bf16[128,768]{1,0:T(8,128)(2,1)}, u32[]{:S(2)}) %copy-start.1) | copy-done | bytes 196632
  3.5 0.0 copy-start.2
  3.5 0.9 %copy-done.2 = bf16[128,768]{1,0:T(8,128)(2,1)S(1)} copy-done((bf16[128,768]{1,0:T(8,128)(2,1)S(1)}, bf16[128,768]{1,0:T(8,128)(2,1)}, u32[]{:S(2)}) %copy-start.2) | copy-done | bytes 196632
  4.4 0.0 copy-start.3
  4.4 0.9 %copy-done.3 = bf16[128,768]{1,0:T(8,128)(2,1)S(1)} copy-done((bf16[128,768]{1,0:T(8,128)(2,1)S(1)}, bf16[128,768]{1,0:T(8,128)(2,1)}, u32[]{:S(2)}) %copy-start.3) | copy-done | bytes 196632
  5.3 0.0 copy-start.4
  5.3 0.9 %copy-done.4 = bf16[128,768]{1,0:T(8,128)(2,1)S(1)} copy-done((bf16[128,768]{1,0:T(8,128)(2,1)S(1)}, bf16[128,768]{1,0:T(8,128)(2,1)}, u32[]{:S(2)}) %copy-start.4) | copy-done | bytes 196632
  6.2 0.0 copy-start.5
  6.2 0.9 %copy-done.5 = bf16[768,96]{0,1:T(8,128)(2,1)S(1)} copy-done((bf16[768,96]{0,1:T(8,128)(2,1)S(1)}, bf16[768,96]{0,1:T(8,128)(2,1)}, u32[]{:S(2)}) %copy-start.5) | copy-done | bytes 147480
  7.1 0.0 copy-start.6
  7.1 0.9 %copy-done.6 = bf16[256,256]{1,0:T(8,128)(2,1)S(1)} copy-done((bf16[256,256]{1,0:T(8,128)(2,1)S(1)}, bf16[256,256]{1,0:T(8,128)(2,1)}, u32[]{:S(2)}) %copy-start.6) | copy-done | bytes 131096
  8.0 0.0 copy-start.7
  8.1 0.9 %copy-done.7 = bf16[256,256]{1,0:T(8,128)(2,1)S(1)} copy-done((bf16[256,256]{1,0:T(8,128)(2,1)S(1)}, bf16[256,256]{1,0:T(8,128)(2,1)}, u32[]{:S(2)}) %copy-start.7) | copy-done | bytes 131096
  9.0 0.0 copy-start.8
  9.0 0.8 %copy-done.8 = bf16[256,128]{1,0:T(8,128)(2,1)S(1)} copy-done((bf16[256,128]{1,0:T(8,128)(2,1)S(1)}, bf16[256,128]{1,0:T(8,128)(2,1)}, u32[]{:S(2)}) %copy-start.8) | copy-done | bytes 65560
  9.8 60.2 %shard_map.120 = (bf16[768,128]{1,0:T(8,128)(2,1)S(1)}, bf16[128,768]{1,0:T(8,128)(2,1)S(1)}, f32[768,128]{1,0:T(8,128)S(1)}, f32[96,768]{1,0:T(8,128)S(1)}) custom-call(bf16[128,768]{1,0:T(8,128)(2,1)S(1)} %copy-done.1, bf16[96,768]{1,0:T(8,128)(2,1)S(1)} %bitcast.7, bf16[128,768]{1,0:T(8,128)(2,1)S(1)} %copy-done.2, bf16[128,768]{1,0:T(8,128)(2,1)S(1)} %copy-done.3, ...), custom_call_target="tpu_custom_call" | custom-call | tf_op jit(solution)/shard_map/pallas_call | solution.py:390
  70.0 0.8 %copy.13 = bf16[128,768]{1,0:T(8,128)(2,1)} copy(bf16[128,768]{0,1:T(8,128)(2,1)S(1)} %bitcast.6) | data formatting | bytes 393216
  70.8 0.9 %copy.14 = f32[128,768]{1,0:T(8,128)} copy(f32[128,768]{0,1:T(8,128)S(1)} %bitcast.4) | data formatting | bytes 786432
  71.8 0.7 copy.17
  72.4 0.7 copy.18
Async XLA Ops:
  0.6 1.9 %copy-start = (bf16[768,2048]{1,0:T(8,128)(2,1)S(1)}, bf16[768,2048]{1,0:T(8,128)(2,1)}, u32[]{:S(2)}) copy-start(bf16[768,2048]{1,0:T(8,128)(2,1)} %taps_ref.1) | copy-start | bytes 9437188
  2.5 0.9 %copy-start.1 = (bf16[128,768]{1,0:T(8,128)(2,1)S(1)}, bf16[128,768]{1,0:T(8,128)(2,1)}, u32[]{:S(2)}) copy-start(bf16[128,768]{1,0:T(8,128)(2,1)} %cot_ref.1) | copy-start | bytes 589828
  3.5 0.9 %copy-start.2 = (bf16[128,768]{1,0:T(8,128)(2,1)S(1)}, bf16[128,768]{1,0:T(8,128)(2,1)}, u32[]{:S(2)}) copy-start(bf16[128,768]{1,0:T(8,128)(2,1)} %val_ref.1) | copy-start | bytes 589828
  4.4 0.9 %copy-start.3 = (bf16[128,768]{1,0:T(8,128)(2,1)S(1)}, bf16[128,768]{1,0:T(8,128)(2,1)}, u32[]{:S(2)}) copy-start(bf16[128,768]{1,0:T(8,128)(2,1)} %gate_ref.1) | copy-start | bytes 589828
  5.3 0.9 %copy-start.4 = (bf16[128,768]{1,0:T(8,128)(2,1)S(1)}, bf16[128,768]{1,0:T(8,128)(2,1)}, u32[]{:S(2)}) copy-start(bf16[128,768]{1,0:T(8,128)(2,1)} %conv_ref.1) | copy-start | bytes 589828
  6.2 0.9 %copy-start.5 = (bf16[768,96]{0,1:T(8,128)(2,1)S(1)}, bf16[768,96]{0,1:T(8,128)(2,1)}, u32[]{:S(2)}) copy-start(bf16[768,96]{0,1:T(8,128)(2,1)} %param.10) | copy-start | bytes 442372
  7.1 0.9 %copy-start.6 = (bf16[256,256]{1,0:T(8,128)(2,1)S(1)}, bf16[256,256]{1,0:T(8,128)(2,1)}, u32[]{:S(2)}) copy-start(bf16[256,256]{1,0:T(8,128)(2,1)} %constant.8.clone.lback_hbm) | copy-start | bytes 393220
  8.0 0.9 %copy-start.7 = (bf16[256,256]{1,0:T(8,128)(2,1)S(1)}, bf16[256,256]{1,0:T(8,128)(2,1)}, u32[]{:S(2)}) copy-start(bf16[256,256]{1,0:T(8,128)(2,1)} %constant.6.clone.fwd_hbm) | copy-start | bytes 393220
  9.0 0.8 %copy-start.8 = (bf16[256,128]{1,0:T(8,128)(2,1)S(1)}, bf16[256,128]{1,0:T(8,128)(2,1)}, u32[]{:S(2)}) copy-start(bf16[256,128]{1,0:T(8,128)(2,1)} %constant.7.clone.vback_hbm) | copy-start | bytes 196612

commit v3 on v2

--- a/solution.py
+++ b/solution.py
@@ -229,6 +229,7 @@
     for copy in local:
         copy.wait()
     gated_all[q] = (gate_in[...].astype(f32) * conv_in[...].astype(f32)).astype(bf16)
+    go(send(gated_all.at[q], gated_all.at[q], gts.at[2], gtr.at[2], at(0, 2)))
     go(send(gated_all.at[q], gated_all.at[q], gts.at[1], gtr.at[1], at(0, 1)))
     valt[...] = val_in[...].astype(f32).T.astype(bf16).reshape(n, group, rows)
 
@@ -240,37 +241,33 @@
         go(send(slot, slot, wys.at[level], wyr.at[level], at(0, 2)))
         go(send(slot, slot, wcs.at[level], wcr.at[level], at(0, 1)))
 
+    lane = lax.broadcasted_iota(jnp.int32, (n, group, rows), 2)
+
+    def split(spec, re_ref, im_ref, mix_ref, sign):
+        real = spec[:, :rows].reshape(n, group, rows)
+        imag = spec[:, rows:].reshape(n, group, rows)
+        re_ref[...] = real
+        if mix_ref is None:
+            im_ref[...] = imag
+        else:
+            im_ref[...] = jnp.where(lane == 0, 0.0, imag)
+            mix_ref[...] = jnp.where(lane == 0, sign * imag, real)
+
+    def spectra(source, re_ref, im_ref, mix_ref):
+        blocks = source[...].reshape(n * group, rows)
+        spec = jnp.dot(blocks, fwd_ref[:rows, :], preferred_element_type=f32)
+        split(spec, re_ref, im_ref, mix_ref, 1.0)
+
+    windows = jnp.concatenate(
+        [taps[:, m * rows:(m + 2) * rows] for m in range(n)], axis=0
+    )
+    spec = jnp.dot(windows, fwd_ref[...], preferred_element_type=f32)
+    split(spec, tre, tim, tmix, -1.0)
+
     weight_from(1)
     weight_from(2)
-
-    lane = lax.broadcasted_iota(jnp.int32, (group, rows), 1)
-
-    def split(spec, re_ref, im_ref, mix_ref, j, sign):
-        real, imag = spec[:, :rows], spec[:, rows:]
-        re_ref[j] = real
-        if mix_ref is None:
-            im_ref[j] = imag
-        else:
-            im_ref[j] = jnp.where(lane == 0, 0.0, imag)
-            mix_ref[j] = jnp.where(lane == 0, sign * imag, real)
-
-    def spectra(source, re_ref, im_ref, mix_ref):
-        def one(j, carry):
-            spec = jnp.dot(source[j], fwd_ref[:rows, :], preferred_element_type=f32)
-            split(spec, re_ref, im_ref, mix_ref, j, 1.0)
-            return carry
-        lax.fori_loop(0, n, one, 0, unroll=4)
-
-    for m in range(n):
-        spec = jnp.dot(
-            taps[:, m * rows:(m + 2) * rows], fwd_ref[...], preferred_element_type=f32
-        )
-        split(spec, tre, tim, tmix, m, -1.0)
-
     weight_from(3)
     all_to_all(valt, valr, vs, vr)
-    go(send(gated_all.at[q], gated_all.at[q], gts.at[2], gtr.at[2], at(0, 2)))
-
     x_copy.wait_recv()
     for part in range(2):
         turned = feat[part].astype(f32).T.astype(bf16)
@@ -308,19 +305,18 @@
             send(there, there, gts.at[k], gtr.at[k], at(0, k)).wait_recv()
         send(featq.at[q], featr.at[quad[k]], fts.at[k], ftr.at[k], at(0, k)).wait_recv()
 
-    def weight_part(level):
-        z = levels[level]
-        total = jnp.dot(featr[0, z], gated_all[0], preferred_element_type=f32)
-        for k in range(1, 4):
-            total = total + jnp.dot(featr[k, z], gated_all[k], preferred_element_type=f32)
-        return total
-
-    pair_out[0] = weight_part(3).astype(bf16)
+    slices, width = featr.shape[2], gated_all.shape[2]
+    tokens = jnp.concatenate(
+        [featr[k].reshape(nz * slices, rows) for k in range(4)], axis=1
+    )
+    pw[...] = jnp.dot(
+        tokens, gated_all[...].reshape(4 * rows, width), preferred_element_type=f32
+    ).reshape(nz, slices, width)
+
+    pair_out[0] = pw[levels[3]].astype(bf16)
     go(send(pair_out.at[0], pair_in.at[0], rs.at[0], rr.at[0], at(2, 0)))
-    pair_out[1] = weight_part(2).astype(bf16)
+    pair_out[1] = pw[levels[2]].astype(bf16)
     go(send(pair_out.at[1], pair_in.at[1], rs.at[1], rr.at[1], at(2, 0)))
-    pw[0] = weight_part(1)
-    pw[1] = weight_part(0)
 
     arrive(valt, valr, vs, vr)
     spectra(valr, vre, vim, vmix)
@@ -344,7 +340,7 @@
     all_to_all(gvt, gvr, os, orr)
 
     send(pair_out.at[0], pair_in.at[0], rs.at[0], rr.at[0], at(2, 0)).wait_recv()
-    cross_out[...] = (pw[0] + pair_in[0].astype(f32)).astype(bf16)
+    cross_out[...] = (pw[levels[1]] + pair_in[0].astype(f32)).astype(bf16)
     go(send(cross_out, cross_in, rs.at[2], rr.at[2], at(1, 0)))
 
     def lag_rows(r, carry):
@@ -366,13 +362,20 @@
 
     send(pair_out.at[1], pair_in.at[1], rs.at[1], rr.at[1], at(2, 0)).wait_recv()
     send(cross_out, cross_in, rs.at[2], rr.at[2], at(1, 0)).wait_recv()
-    gw_ref[...] = pw[1] + pair_in[1].astype(f32) + cross_in[...].astype(f32)
+    gw_ref[...] = pw[zi] + pair_in[1].astype(f32) + cross_in[...].astype(f32)
     arrive(gvt, gvr, os, orr)
     gv_ref[...] = gvr[...].reshape(n * group, rows)
     arrive(gft, gfr, ls, lr)
-    gf_ref[...] = gfr[...].reshape(n * group, rows).astype(f32)
+    gf_ref[...] = gfr[...].reshape(n * group, rows)
     for copy in pending:
         copy.wait_send()
+
+
+def finish_kernel(gv_ref, gg_ref, gf_ref, gw_ref, gv_out, gg_out, gf_out, gw_out):
+    gv_out[...] = gv_ref[...].astype(jnp.float32).T.astype(jnp.bfloat16)
+    gg_out[...] = gg_ref[...]
+    gf_out[...] = gf_ref[...].astype(jnp.float32).T
+    gw_out[...] = gw_ref[...]
 
 
 def split_body(cotangent, out_weight, values, gate_input, conv_out, filter_taps):
@@ -392,7 +395,7 @@
         out_shape=(
             jax.ShapeDtypeStruct((channels, rows), bf16),
             jax.ShapeDtypeStruct((rows, channels), bf16),
-            jax.ShapeDtypeStruct((channels, rows), f32),
+            jax.ShapeDtypeStruct((channels, rows), bf16),
             jax.ShapeDtypeStruct((slice_cols, channels), f32),
         ),
         in_specs=[pl.BlockSpec(memory_space=pltpu.HBM)] * 9,
@@ -411,7 +414,7 @@
         ] + [vm(trip, f32)] * 8 + [
             vm((n, group, 2 * rows), f32),
             vm((n, group, 2 * rows), f32),
-            vm((2, slice_cols, channels), f32),
+            vm((nz, slice_cols, channels), f32),
             vm((2, slice_cols, channels), bf16),
             vm((2, slice_cols, channels), bf16),
             vm((slice_cols, channels), bf16),
@@ -421,13 +424,25 @@
             dma((4,)), dma((4,)), dma((4,)), dma((4,)),
         ] + [dma((n,))] * 8 + [dma((3,)), dma((3,)), dma((9,))],
         compiler_params=pltpu.CompilerParams(
-            collective_id=0, has_side_effects=True, vmem_limit_bytes=48 * 1024 * 1024
+            collective_id=0, has_side_effects=True, vmem_limit_bytes=60 * 1024 * 1024
         ),
     )(
         cotangent, out_weight.T, values, gate_input, conv_out, filter_taps,
         forward, value_back, lag_back,
     )
-    return gv.T, gg, gf.T, gw.T
+    gv, gg, gf, gw = pl.pallas_call(
+        finish_kernel,
+        out_shape=(
+            jax.ShapeDtypeStruct((rows, channels), bf16),
+            jax.ShapeDtypeStruct((rows, channels), bf16),
+            jax.ShapeDtypeStruct((rows, channels), f32),
+            jax.ShapeDtypeStruct((slice_cols, channels), f32),
+        ),
+        in_specs=[vmem] * 4,
+        out_specs=(vmem,) * 4,
+        compiler_params=pltpu.CompilerParams(vmem_limit_bytes=60 * 1024 * 1024),
+    )(gv, gg, gf, gw)
+    return gv, gg, gf, gw.T
 
 
 def solution(mesh):

time: 73.5 us -> 58.4 us (0.79)
  local copies, waits for them, and re-layouts: 12.3 us -> 0 us
  Pallas kernels: 60.2 us -> 57.7 us
    unnamed x22 -> x0, local copies, waits for them, and re-layouts: 12.3 us -> none
    pallas_call x1, Pallas kernels: 60.2 us -> 55.3 us  [split_body(): pl.pallas_call(functools.partial(mixer_kernel, n, nz), out_shape=(jax.Sha...]
    pallas_call x0 -> x1, Pallas kernels: none -> 2.34 us  [split_body(): pl.pallas_call(finish_kernel, out_shape=(jax.ShapeDtypeStruct((rows, chan...]
where the time goes in v3:
time: 58.4 us; the launch traced here: 58.3 us
  Pallas kernels  57.7 us (99%)
  between operations  0.64 us (1%)
    pallas_call x1, Pallas kernels, split_body(): pl.pallas_call(functools.partial(mixer_kernel, n, nz), out_shape=(jax.Sha...  55.3 us
    pallas_call x1, Pallas kernels, split_body(): pl.pallas_call(finish_kernel, out_shape=(jax.ShapeDtypeStruct((rows, chan...  2.34 us

profile of v3, /device:TPU:0, one launch (start us, length us, event | category | flops | bytes accessed | tf_op | source)
XLA Modules:
  0.0 58.3 jit_solution(18050631011538333675)
XLA Ops:
  0.6 55.3 %shard_map.120 = (bf16[768,128]{1,0:T(8,128)(2,1)}, bf16[128,768]{1,0:T(8,128)(2,1)}, bf16[768,128]{1,0:T(8,128)(2,1)}, f32[96,768]{1,0:T(8,128)}) custom-call(bf16[128,768]{1,0:T(8,128)(2,1)} %cot_ref.1, bf16[96,768]{1,0:T(8,128)(2,1)} %bitcast.2, bf16[128,768]{1,0:T(8,128)(2,1)} %val_ref.1, bf16[128,768]{1,0:T(8,128)(2,1)} %gate_ref.1, ...), custom_call_target="tpu_custom_call" | custom-call | tf_op jit(solution)/shard_map/pallas_call | solution.py:393
  56.0 2.3 %shard_map.121 = (bf16[128,768]{1,0:T(8,128)(2,1)}, bf16[128,768]{1,0:T(8,128)(2,1)}, f32[128,768]{1,0:T(8,128)}, f32[96,768]{1,0:T(8,128)}) custom-call(bf16[768,128]{1,0:T(8,128)(2,1)} %get-tuple-element.12.gv_ref, bf16[128,768]{1,0:T(8,128)(2,1)} %get-tuple-element.13.gg_ref, bf16[768,128]{1,0:T(8,128)(2,1)} %get-tuple-element.14.gf_ref, ...), custom_call_target="tpu_custom_call" | custom-call | tf_op jit(solution)/shard_map/pallas_call | solution.py:433

commit v4 on v3

--- a/solution.py
+++ b/solution.py
@@ -150,7 +150,8 @@
     val_in, gate_in, conv_in, fwd_ref, vback_ref, lback_ref,
     feat, wall, gated_all, featq, featr, valt, valr, gct, gcr, gvt, gvr, gft, gfr,
     taps, cre, cim, tre, tim, tmix, vre, vim, vmix, sums, lags, pw, pair_out, pair_in, cross_out, cross_in,
-    xsem, wzs, wzr, wys, wyr, wcs, wcr, gts, gtr, fts, ftr, vs, vr, cs, cr, os, orr, ls, lr, rs, rr, tsem,
+    shares, core_in, y_out, y_in,
+    xsem, wzs, wzr, ms, mr, gts, gtr, fts, ftr, vs, vr, cs, cr, os, orr, ls, lr, rs, rr, tsem,
 ):
     rows = val_in.shape[0]
     group = gct.shape[1]
@@ -178,7 +179,7 @@
 
     local = [
         pltpu.make_async_copy(src, dst, tsem.at[i]) for i, (src, dst) in enumerate([
-            (wt_ref, wall.at[me]),
+            (wt_ref, wall.at[zi]),
             (cot_ref, feat.at[fs]),
             (gate_ref, gate_in),
             (conv_ref, conv_in),
@@ -208,12 +209,10 @@
         pending.append(copy)
         return copy
 
-    own = wall.at[me]
+    own = wall.at[zi]
+    x_copy = go(send(cot_ref, feat.at[fs], xsem.at[0], xsem.at[1], me, 1 - fs))
     go(send(wt_ref, own, wzs.at[1], wzr.at[1], at(1, 0)))
     go(send(wt_ref, own, wzs.at[2], wzr.at[2], at(2, 0)))
-    go(send(wt_ref, own, wys.at[0], wyr.at[0], at(0, 2)))
-    x_copy = go(send(cot_ref, feat.at[fs], xsem.at[0], xsem.at[1], me, 1 - fs))
-    go(send(wt_ref, own, wcs.at[0], wcr.at[0], at(0, 1)))
 
     def all_to_all(src, dst, send_sems, recv_sems):
         dst[me] = src[me]
@@ -234,12 +233,10 @@
     valt[...] = val_in[...].astype(f32).T.astype(bf16).reshape(n, group, rows)
 
     def weight_from(level):
-        slot = wall.at[at(level, 0)]
+        slot = wall.at[levels[level]]
         send(slot, slot, wzs.at[level], wzr.at[level], at(level, 0)).wait_recv()
         if level == 1:
             go(send(slot, slot, wzs.at[3], wzr.at[3], at(2, 0)))
-        go(send(slot, slot, wys.at[level], wyr.at[level], at(0, 2)))
-        go(send(slot, slot, wcs.at[level], wcr.at[level], at(0, 1)))
 
     lane = lax.broadcasted_iota(jnp.int32, (n, group, rows), 2)
 
@@ -258,16 +255,6 @@
         spec = jnp.dot(blocks, fwd_ref[:rows, :], preferred_element_type=f32)
         split(spec, re_ref, im_ref, mix_ref, 1.0)
 
-    windows = jnp.concatenate(
-        [taps[:, m * rows:(m + 2) * rows] for m in range(n)], axis=0
-    )
-    spec = jnp.dot(windows, fwd_ref[...], preferred_element_type=f32)
-    split(spec, tre, tim, tmix, -1.0)
-
-    weight_from(1)
-    weight_from(2)
-    weight_from(3)
-    all_to_all(valt, valr, vs, vr)
     x_copy.wait_recv()
     for part in range(2):
         turned = feat[part].astype(f32).T.astype(bf16)
@@ -276,39 +263,44 @@
             s = part * (n // 2) + j
             featq[s % 4, s // 4] = turned[j * per:(j + 1) * per]
     featr[q] = featq[q]
+    for k in (2, 3, 1):
+        go(send(featq.at[quad[k]], featr.at[q], fts.at[k], ftr.at[k], at(0, k)))
+    weight_from(1)
+
+    windows = jnp.concatenate(
+        [taps[:, m * rows:(m + 2) * rows] for m in range(n)], axis=0
+    )
+    spec = jnp.dot(windows, fwd_ref[...], preferred_element_type=f32)
+    split(spec, tre, tim, tmix, -1.0)
+
     for k in range(1, 4):
-        go(send(featq.at[quad[k]], featr.at[q], fts.at[k], ftr.at[k], at(0, k)))
-
-    for level in range(nz):
-        slot = wall.at[at(level, 2)]
-        send(slot, slot, wys.at[level], wyr.at[level], at(0, 2)).wait_recv()
-        go(send(slot, slot, wcs.at[nz + level], wcr.at[nz + level], at(0, 1)))
+        send(featq.at[q], featr.at[quad[k]], fts.at[k], ftr.at[k], at(0, k)).wait_recv()
+    slices, width = featr.shape[2], gated_all.shape[2]
+    tokens = jnp.concatenate(
+        [featr[k].reshape(nz * slices, rows) for k in range(4)], axis=1
+    )
+    weight_from(2)
+    weight_from(3)
+    partial = jnp.dot(
+        tokens.astype(f32).T.astype(bf16),
+        wall[...].reshape(nz * slices, width),
+        preferred_element_type=f32,
+    )
+    for k in range(4):
+        shares[k % 2, k // 2] = partial[k * rows:(k + 1) * rows]
+    core_copy = go(send(shares.at[1 - core], core_in, ms.at[0], mr.at[0], at(0, 1)))
+
     far_gated = gated_all.at[quad[2]]
     send(far_gated, far_gated, gts.at[2], gtr.at[2], at(0, 2)).wait_recv()
     go(send(far_gated, far_gated, gts.at[3], gtr.at[3], at(0, 1)))
-    for k in range(2 * nz):
-        slot = wall.at[at(k % nz, 1 if k < nz else 3)]
-        send(slot, slot, wcs.at[k], wcr.at[k], at(0, 1)).wait_recv()
-
-    half = n // 2
-    width = wall.shape[2]
-    mixed = jnp.dot(
-        feat[0], wall[:half].reshape(-1, width), preferred_element_type=f32
-    ) + jnp.dot(feat[1], wall[half:].reshape(-1, width), preferred_element_type=f32)
-    gct[...] = (mixed * gate_in[...].astype(f32)).T.astype(bf16).reshape(n, group, rows)
-    all_to_all(gct, gcr, cs, cr)
-    gg_ref[...] = (mixed * conv_in[...].astype(f32)).astype(bf16)
-
-    for k in range(1, 4):
+
+    core_copy.wait_recv()
+    y_out[...] = (shares[core, 1 - y] + core_in[1 - y]).astype(bf16)
+    y_copy = go(send(y_out, y_in, ms.at[1], mr.at[1], at(0, 2)))
+
+    for k in (1, 3):
         there = gated_all.at[quad[k]]
-        if k != 2:
-            send(there, there, gts.at[k], gtr.at[k], at(0, k)).wait_recv()
-        send(featq.at[q], featr.at[quad[k]], fts.at[k], ftr.at[k], at(0, k)).wait_recv()
-
-    slices, width = featr.shape[2], gated_all.shape[2]
-    tokens = jnp.concatenate(
-        [featr[k].reshape(nz * slices, rows) for k in range(4)], axis=1
-    )
+        send(there, there, gts.at[k], gtr.at[k], at(0, k)).wait_recv()
     pw[...] = jnp.dot(
         tokens, gated_all[...].reshape(4 * rows, width), preferred_element_type=f32
     ).reshape(nz, slices, width)
@@ -318,10 +310,18 @@
     pair_out[1] = pw[levels[2]].astype(bf16)
     go(send(pair_out.at[1], pair_in.at[1], rs.at[1], rr.at[1], at(2, 0)))
 
-    arrive(valt, valr, vs, vr)
-    spectra(valr, vre, vim, vmix)
+    y_copy.wait_recv()
+    mixed = shares[core, y] + core_in[y] + y_in[...].astype(f32)
+    gct[...] = (mixed * gate_in[...].astype(f32)).T.astype(bf16).reshape(n, group, rows)
+    all_to_all(gct, gcr, cs, cr)
+    gg_ref[...] = (mixed * conv_in[...].astype(f32)).astype(bf16)
+    all_to_all(valt, valr, vs, vr)
+
     arrive(gct, gcr, cs, cr)
     spectra(gcr, cre, cim, None)
+    send(pair_out.at[0], pair_in.at[0], rs.at[0], rr.at[0], at(2, 0)).wait_recv()
+    cross_out[...] = (pw[levels[1]] + pair_in[0].astype(f32)).astype(bf16)
+    go(send(cross_out, cross_in, rs.at[2], rr.at[2], at(1, 0)))
 
     def value_rows(r, carry):
         at_rows = pl.ds(pl.multiple_of(r * 8, 8), 8)
@@ -339,9 +339,8 @@
     gvt[...] = blocks.astype(bf16).reshape(n, group, rows)
     all_to_all(gvt, gvr, os, orr)
 
-    send(pair_out.at[0], pair_in.at[0], rs.at[0], rr.at[0], at(2, 0)).wait_recv()
-    cross_out[...] = (pw[levels[1]] + pair_in[0].astype(f32)).astype(bf16)
-    go(send(cross_out, cross_in, rs.at[2], rr.at[2], at(1, 0)))
+    arrive(valt, valr, vs, vr)
+    spectra(valr, vre, vim, vmix)
 
     def lag_rows(r, carry):
         at_rows = pl.ds(pl.multiple_of(r * 8, 8), 8)
@@ -405,7 +404,7 @@
             vm((2 * rows, rows), bf16),
             vm((2 * rows, 2 * rows), bf16),
             vm((2, rows, channels), bf16),
-            vm((n, slice_cols, channels), bf16),
+            vm((nz, slice_cols, channels), bf16),
             vm((4, rows, channels), bf16),
             vm((4, nz, slice_cols, rows), bf16),
             vm((4, nz, slice_cols, rows), bf16),
@@ -419,8 +418,12 @@
             vm((2, slice_cols, channels), bf16),
             vm((slice_cols, channels), bf16),
             vm((slice_cols, channels), bf16),
+            vm((2, 2, rows, channels), f32),
+            vm((2, rows, channels), f32),
+            vm((rows, channels), bf16),
+            vm((rows, channels), bf16),
             dma((2,)),
-            dma((nz,)), dma((nz,)), dma((nz,)), dma((nz,)), dma((2 * nz,)), dma((2 * nz,)),
+            dma((nz,)), dma((nz,)), dma((2,)), dma((2,)),
             dma((4,)), dma((4,)), dma((4,)), dma((4,)),
         ] + [dma((n,))] * 8 + [dma((3,)), dma((3,)), dma((9,))],
         compiler_params=pltpu.CompilerParams(

time: 58.4 us -> 57.4 us (0.983)
  Pallas kernels: 57.7 us -> 56.7 us
    pallas_call x1, Pallas kernels: 55.3 us -> 54.3 us  [split_body(): pl.pallas_call(functools.partial(mixer_kernel, n, nz), out_shape=(jax.Sha...]
where the time goes in v4:
time: 57.4 us; the launch traced here: 57.3 us
  Pallas kernels  56.7 us (99%)
  between operations  0.64 us (1%)
    pallas_call x1, Pallas kernels, split_body(): pl.pallas_call(functools.partial(mixer_kernel, n, nz), out_shape=(jax.Sha...  54.3 us
    pallas_call x1, Pallas kernels, split_body(): pl.pallas_call(finish_kernel, out_shape=(jax.ShapeDtypeStruct((rows, chan...  2.34 us

profile of v4, /device:TPU:0, one launch (start us, length us, event | category | flops | bytes accessed | tf_op | source)
XLA Modules:
  0.0 57.3 jit_solution(7961324585297172353)
XLA Ops:
  0.6 54.3 %shard_map.120 = (bf16[768,128]{1,0:T(8,128)(2,1)}, bf16[128,768]{1,0:T(8,128)(2,1)}, bf16[768,128]{1,0:T(8,128)(2,1)}, f32[96,768]{1,0:T(8,128)}) custom-call(bf16[128,768]{1,0:T(8,128)(2,1)} %cot_ref.1, bf16[96,768]{1,0:T(8,128)(2,1)} %bitcast.2, bf16[128,768]{1,0:T(8,128)(2,1)} %val_ref.1, bf16[128,768]{1,0:T(8,128)(2,1)} %gate_ref.1, ...), custom_call_target="tpu_custom_call" | custom-call | tf_op jit(solution)/shard_map/pallas_call | solution.py:392
  55.0 2.3 %shard_map.121 = (bf16[128,768]{1,0:T(8,128)(2,1)}, bf16[128,768]{1,0:T(8,128)(2,1)}, f32[128,768]{1,0:T(8,128)}, f32[96,768]{1,0:T(8,128)}) custom-call(bf16[768,128]{1,0:T(8,128)(2,1)} %get-tuple-element.12.gv_ref, bf16[128,768]{1,0:T(8,128)(2,1)} %get-tuple-element.13.gg_ref, bf16[768,128]{1,0:T(8,128)(2,1)} %get-tuple-element.14.gf_ref, ...), custom_call_target="tpu_custom_call" | custom-call | tf_op jit(solution)/shard_map/pallas_call | solution.py:436

commit v5 on v4

--- a/solution.py
+++ b/solution.py
@@ -151,7 +151,7 @@
     feat, wall, gated_all, featq, featr, valt, valr, gct, gcr, gvt, gvr, gft, gfr,
     taps, cre, cim, tre, tim, tmix, vre, vim, vmix, sums, lags, pw, pair_out, pair_in, cross_out, cross_in,
     shares, core_in, y_out, y_in,
-    xsem, wzs, wzr, ms, mr, gts, gtr, fts, ftr, vs, vr, cs, cr, os, orr, ls, lr, rs, rr, tsem,
+    xsem, wzs, wzr, ms, mr, gts, gtr, fts, ftr, vs, cs, os, ls, rs, rr, tsem,
 ):
     rows = val_in.shape[0]
     group = gct.shape[1]
@@ -214,16 +214,20 @@
     go(send(wt_ref, own, wzs.at[1], wzr.at[1], at(1, 0)))
     go(send(wt_ref, own, wzs.at[2], wzr.at[2], at(2, 0)))
 
-    def all_to_all(src, dst, send_sems, recv_sems):
-        dst[me] = src[me]
+    def whole(src, dst, sems):
+        others = pl.ds(0, n - 1)
+        to = lax.rem(me + 1, n)
+        return send(src.at[others], dst.at[others], sems.at[0], sems.at[1], to)
+
+    def all_to_all(src, dst, sems):
         for k in range(1, n):
             to = lax.rem(me + k, n)
-            go(send(src.at[to], dst.at[me], send_sems.at[k], recv_sems.at[k], to))
-
-    def arrive(src, dst, send_sems, recv_sems):
-        for k in range(1, n):
-            origin = lax.rem(me + n - k, n)
-            send(src.at[me], dst.at[origin], send_sems.at[k], recv_sems.at[k], origin).wait_recv()
+            send(src.at[to], dst.at[me], sems.at[0], sems.at[1], to).start()
+        dst[me] = src[me]
+        pending.append(whole(src, dst, sems))
+
+    def arrive(src, dst, sems):
+        whole(src, dst, sems).wait_recv()
 
     for copy in local:
         copy.wait()
@@ -313,43 +317,66 @@
     y_copy.wait_recv()
     mixed = shares[core, y] + core_in[y] + y_in[...].astype(f32)
     gct[...] = (mixed * gate_in[...].astype(f32)).T.astype(bf16).reshape(n, group, rows)
-    all_to_all(gct, gcr, cs, cr)
+    all_to_all(gct, gcr, cs)
     gg_ref[...] = (mixed * conv_in[...].astype(f32)).astype(bf16)
-    all_to_all(valt, valr, vs, vr)
-
-    arrive(gct, gcr, cs, cr)
+    all_to_all(valt, valr, vs)
+
+    arrive(gct, gcr, cs)
     spectra(gcr, cre, cim, None)
     send(pair_out.at[0], pair_in.at[0], rs.at[0], rr.at[0], at(2, 0)).wait_recv()
     cross_out[...] = (pw[levels[1]] + pair_in[0].astype(f32)).astype(bf16)
     go(send(cross_out, cross_in, rs.at[2], rr.at[2], at(1, 0)))
 
+    block = 4
+
+    def load(refs, j, at_rows):
+        return tuple(ref[j, at_rows, :] for ref in refs)
+
     def value_rows(r, carry):
         at_rows = pl.ds(pl.multiple_of(r * 8, 8), 8)
-        for i in range(n):
-            c_re, c_im = cre[i:n, at_rows, :], cim[i:n, at_rows, :]
-            t_re, t_im = tre[:n - i, at_rows, :], tim[:n - i, at_rows, :]
-            t_mix = tmix[:n - i, at_rows, :]
-            sums[i, at_rows, :rows] = jnp.sum(c_re * t_re + c_im * t_im, axis=0)
-            sums[i, at_rows, rows:] = jnp.sum(c_re * t_im - c_im * t_mix, axis=0)
+        for base in range(0, n, block):
+            real, imag, held = {}, {}, {}
+            for j in range(base, n):
+                c_re, c_im = load((cre, cim), j, at_rows)
+                for i in range(base, min(base + block, j + 1)):
+                    m = j - i
+                    if m not in held:
+                        held[m] = load((tre, tim, tmix), m, at_rows)
+                    t_re, t_im, t_mix = held[m]
+                    re, im = c_re * t_re + c_im * t_im, c_re * t_im - c_im * t_mix
+                    real[i] = real[i] + re if i in real else re
+                    imag[i] = imag[i] + im if i in imag else im
+            for i in range(base, base + block):
+                sums[i, at_rows, :rows] = real[i]
+                sums[i, at_rows, rows:] = imag[i]
         return carry
 
     lax.fori_loop(0, group // 8, value_rows, 0)
     packed = sums[...].astype(bf16).reshape(n * group, 2 * rows)
     blocks = jnp.dot(packed, vback_ref[...], preferred_element_type=f32)
     gvt[...] = blocks.astype(bf16).reshape(n, group, rows)
-    all_to_all(gvt, gvr, os, orr)
-
-    arrive(valt, valr, vs, vr)
+    all_to_all(gvt, gvr, os)
+
+    arrive(valt, valr, vs)
     spectra(valr, vre, vim, vmix)
 
     def lag_rows(r, carry):
         at_rows = pl.ds(pl.multiple_of(r * 8, 8), 8)
-        for m in range(n):
-            c_re, c_im = cre[m:n, at_rows, :], cim[m:n, at_rows, :]
-            v_re, v_im = vre[:n - m, at_rows, :], vim[:n - m, at_rows, :]
-            v_mix = vmix[:n - m, at_rows, :]
-            lags[m, at_rows, :rows] = jnp.sum(v_re * c_re + v_im * c_im, axis=0)
-            lags[m, at_rows, rows:] = jnp.sum(v_mix * c_im - v_im * c_re, axis=0)
+        for base in range(0, n, block):
+            real, imag, held = {}, {}, {}
+            for i in range(n - base):
+                v_re, v_im, v_mix = load((vre, vim, vmix), i, at_rows)
+                for m in range(base, min(base + block, n - i)):
+                    j = i + m
+                    if j not in held:
+                        held[j] = load((cre, cim), j, at_rows)
+                    c_re, c_im = held[j]
+                    re, im = v_re * c_re + v_im * c_im, v_mix * c_im - v_im * c_re
+                    real[m] = real[m] + re if m in real else re
+                    imag[m] = imag[m] + im if m in imag else im
+            for m in range(base, base + block):
+                lags[m, at_rows, :rows] = real[m]
+                lags[m, at_rows, rows:] = imag[m]
         return carry
 
     lax.fori_loop(0, group // 8, lag_rows, 0)
@@ -357,14 +384,14 @@
     parts = jnp.dot(packed, lback_ref[...], preferred_element_type=f32)
     first = jnp.concatenate([parts[group:, :rows], jnp.zeros((group, rows), f32)], axis=0)
     gft[...] = (parts[:, rows:] + first).astype(bf16).reshape(n, group, rows)
-    all_to_all(gft, gfr, ls, lr)
+    all_to_all(gft, gfr, ls)
 
     send(pair_out.at[1], pair_in.at[1], rs.at[1], rr.at[1], at(2, 0)).wait_recv()
     send(cross_out, cross_in, rs.at[2], rr.at[2], at(1, 0)).wait_recv()
     gw_ref[...] = pw[zi] + pair_in[1].astype(f32) + cross_in[...].astype(f32)
-    arrive(gvt, gvr, os, orr)
+    arrive(gvt, gvr, os)
     gv_ref[...] = gvr[...].reshape(n * group, rows)
-    arrive(gft, gfr, ls, lr)
+    arrive(gft, gfr, ls)
     gf_ref[...] = gfr[...].reshape(n * group, rows)
     for copy in pending:
         copy.wait_send()
@@ -425,7 +452,7 @@
             dma((2,)),
             dma((nz,)), dma((nz,)), dma((2,)), dma((2,)),
             dma((4,)), dma((4,)), dma((4,)), dma((4,)),
-        ] + [dma((n,))] * 8 + [dma((3,)), dma((3,)), dma((9,))],
+        ] + [dma((2,))] * 4 + [dma((3,)), dma((3,)), dma((9,))],
         compiler_params=pltpu.CompilerParams(
             collective_id=0, has_side_effects=True, vmem_limit_bytes=60 * 1024 * 1024
         ),

time: 57.4 us -> 56.4 us (0.983)
  Pallas kernels: 56.7 us -> 55.6 us
    pallas_call x1, Pallas kernels: 54.3 us -> 53.3 us  [split_body(): pl.pallas_call(functools.partial(mixer_kernel, n, nz), out_shape=(jax.Sha...]
where the time goes in v5:
time: 56.4 us; the launch traced here: 56.3 us
  Pallas kernels  55.6 us (99%)
  between operations  0.64 us (1%)
    pallas_call x1, Pallas kernels, split_body(): pl.pallas_call(functools.partial(mixer_kernel, n, nz), out_shape=(jax.Sha...  53.3 us
    pallas_call x1, Pallas kernels, split_body(): pl.pallas_call(finish_kernel, out_shape=(jax.ShapeDtypeStruct((rows, chan...  2.34 us

profile of v5, /device:TPU:0, one launch (start us, length us, event | category | flops | bytes accessed | tf_op | source)
XLA Modules:
  0.0 56.3 jit_solution(101068598972269345)
XLA Ops:
  0.6 53.3 %shard_map.120 = (bf16[768,128]{1,0:T(8,128)(2,1)}, bf16[128,768]{1,0:T(8,128)(2,1)}, bf16[768,128]{1,0:T(8,128)(2,1)}, f32[96,768]{1,0:T(8,128)}) custom-call(bf16[128,768]{1,0:T(8,128)(2,1)} %cot_ref.1, bf16[96,768]{1,0:T(8,128)(2,1)} %bitcast.2, bf16[128,768]{1,0:T(8,128)(2,1)} %val_ref.1, bf16[128,768]{1,0:T(8,128)(2,1)} %gate_ref.1, ...), custom_call_target="tpu_custom_call" | custom-call | tf_op jit(solution)/shard_map/pallas_call | solution.py:419
  53.9 2.3 %shard_map.121 = (bf16[128,768]{1,0:T(8,128)(2,1)}, bf16[128,768]{1,0:T(8,128)(2,1)}, f32[128,768]{1,0:T(8,128)}, f32[96,768]{1,0:T(8,128)}) custom-call(bf16[768,128]{1,0:T(8,128)(2,1)} %get-tuple-element.12.gv_ref, bf16[128,768]{1,0:T(8,128)(2,1)} %get-tuple-element.13.gg_ref, bf16[768,128]{1,0:T(8,128)(2,1)} %get-tuple-element.14.gf_ref, ...), custom_call_target="tpu_custom_call" | custom-call | tf_op jit(solution)/shard_map/pallas_call | solution.py:463

commit v6 on v5

--- a/solution.py
+++ b/solution.py
@@ -151,7 +151,7 @@
     feat, wall, gated_all, featq, featr, valt, valr, gct, gcr, gvt, gvr, gft, gfr,
     taps, cre, cim, tre, tim, tmix, vre, vim, vmix, sums, lags, pw, pair_out, pair_in, cross_out, cross_in,
     shares, core_in, y_out, y_in,
-    xsem, wzs, wzr, ms, mr, gts, gtr, fts, ftr, vs, cs, os, ls, rs, rr, tsem,
+    wzs, wzr, ms, mr, gts, gtr, fts, ftr, vs, cs, os, ls, rs, rr, tsem,
 ):
     rows = val_in.shape[0]
     group = gct.shape[1]
@@ -180,7 +180,7 @@
     local = [
         pltpu.make_async_copy(src, dst, tsem.at[i]) for i, (src, dst) in enumerate([
             (wt_ref, wall.at[zi]),
-            (cot_ref, feat.at[fs]),
+            (cot_ref, feat),
             (gate_ref, gate_in),
             (conv_ref, conv_in),
             (val_ref, val_in),
@@ -198,9 +198,10 @@
         pl.semaphore_signal(
             barrier, inc=1, device_id=(lax.rem(me + k, n), fs), device_id_type=MESH
         )
-    pl.semaphore_signal(barrier, inc=1, device_id=(me, 1 - fs), device_id_type=MESH)
+    for k in range(4):
+        pl.semaphore_signal(barrier, inc=1, device_id=(at(0, k), 1 - fs), device_id_type=MESH)
     taps[:, :rows] = jnp.zeros((group, rows), bf16)
-    pl.semaphore_wait(barrier, n)
+    pl.semaphore_wait(barrier, n + 3)
 
     pending = []
 
@@ -210,7 +211,6 @@
         return copy
 
     own = wall.at[zi]
-    x_copy = go(send(cot_ref, feat.at[fs], xsem.at[0], xsem.at[1], me, 1 - fs))
     go(send(wt_ref, own, wzs.at[1], wzr.at[1], at(1, 0)))
     go(send(wt_ref, own, wzs.at[2], wzr.at[2], at(2, 0)))
 
@@ -231,6 +231,21 @@
 
     for copy in local:
         copy.wait()
+    halves = nz // 2
+
+    def feature_copy(k, dx):
+        return send(
+            featq.at[quad[k]], featr.at[q, pl.ds(fs * halves, halves)],
+            fts.at[k + 4 * dx], ftr.at[k + 4 * dx], at(0, k), 1 - fs if dx else fs,
+        )
+
+    turned = feat[...].astype(f32).T.astype(bf16)
+    per = turned.shape[0] * 2 // n
+    for j in range(n // 2):
+        featq[j % 4, j // 4] = turned[j * per:(j + 1) * per]
+    for k, dx in ((2, 1), (3, 1), (2, 0), (3, 0), (0, 1), (1, 1), (1, 0)):
+        go(feature_copy(k, dx))
+    featr[q, pl.ds(fs * halves, halves)] = featq[q]
     gated_all[q] = (gate_in[...].astype(f32) * conv_in[...].astype(f32)).astype(bf16)
     go(send(gated_all.at[q], gated_all.at[q], gts.at[2], gtr.at[2], at(0, 2)))
     go(send(gated_all.at[q], gated_all.at[q], gts.at[1], gtr.at[1], at(0, 1)))
@@ -259,16 +274,6 @@
         spec = jnp.dot(blocks, fwd_ref[:rows, :], preferred_element_type=f32)
         split(spec, re_ref, im_ref, mix_ref, 1.0)
 
-    x_copy.wait_recv()
-    for part in range(2):
-        turned = feat[part].astype(f32).T.astype(bf16)
-        per = turned.shape[0] // n * 2
-        for j in range(n // 2):
-            s = part * (n // 2) + j
-            featq[s % 4, s // 4] = turned[j * per:(j + 1) * per]
-    featr[q] = featq[q]
-    for k in (2, 3, 1):
-        go(send(featq.at[quad[k]], featr.at[q], fts.at[k], ftr.at[k], at(0, k)))
     weight_from(1)
 
     windows = jnp.concatenate(
@@ -277,8 +282,12 @@
     spec = jnp.dot(windows, fwd_ref[...], preferred_element_type=f32)
     split(spec, tre, tim, tmix, -1.0)
 
-    for k in range(1, 4):
-        send(featq.at[q], featr.at[quad[k]], fts.at[k], ftr.at[k], at(0, k)).wait_recv()
+    for k, dx in ((1, 0), (2, 0), (3, 0), (0, 1), (1, 1), (2, 1), (3, 1)):
+        half = 1 - fs if dx else fs
+        send(
+            featq.at[q], featr.at[quad[k], pl.ds(half * halves, halves)],
+            fts.at[k + 4 * dx], ftr.at[k + 4 * dx], at(0, k), half,
+        ).wait_recv()
     slices, width = featr.shape[2], gated_all.shape[2]
     tokens = jnp.concatenate(
         [featr[k].reshape(nz * slices, rows) for k in range(4)], axis=1
@@ -430,10 +439,10 @@
             vm((2 * rows, 2 * rows), bf16),
             vm((2 * rows, rows), bf16),
             vm((2 * rows, 2 * rows), bf16),
-            vm((2, rows, channels), bf16),
+            vm((rows, channels), bf16),
             vm((nz, slice_cols, channels), bf16),
             vm((4, rows, channels), bf16),
-            vm((4, nz, slice_cols, rows), bf16),
+            vm((4, nz // 2, slice_cols, rows), bf16),
             vm((4, nz, slice_cols, rows), bf16),
         ] + [vm(trip, bf16)] * 8 + [
             vm((group, (n + 1) * rows), bf16),
@@ -449,9 +458,8 @@
             vm((2, rows, channels), f32),
             vm((rows, channels), bf16),
             vm((rows, channels), bf16),
-            dma((2,)),
             dma((nz,)), dma((nz,)), dma((2,)), dma((2,)),
-            dma((4,)), dma((4,)), dma((4,)), dma((4,)),
+            dma((4,)), dma((4,)), dma((8,)), dma((8,)),
         ] + [dma((2,))] * 4 + [dma((3,)), dma((3,)), dma((9,))],
         compiler_params=pltpu.CompilerParams(
             collective_id=0, has_side_effects=True, vmem_limit_bytes=60 * 1024 * 1024

time: 56.4 us -> 56.6 us (level)
  no operation moved by 1% of the time
where the time goes in v6:
time: 56.6 us; the launch traced here: 56.5 us
  Pallas kernels  55.9 us (99%)
  between operations  0.64 us (1%)
    pallas_call x1, Pallas kernels, split_body(): pl.pallas_call(functools.partial(mixer_kernel, n, nz), out_shape=(jax.Sha...  53.5 us
    pallas_call x1, Pallas kernels, split_body(): pl.pallas_call(finish_kernel, out_shape=(jax.ShapeDtypeStruct((rows, chan...  2.34 us

profile of v6, /device:TPU:0, one launch (start us, length us, event | category | flops | bytes accessed | tf_op | source)
XLA Modules:
  0.0 56.5 jit_solution(10515607544167326792)
XLA Ops:
  0.6 53.5 %shard_map.120 = (bf16[768,128]{1,0:T(8,128)(2,1)}, bf16[128,768]{1,0:T(8,128)(2,1)}, bf16[768,128]{1,0:T(8,128)(2,1)}, f32[96,768]{1,0:T(8,128)}) custom-call(bf16[128,768]{1,0:T(8,128)(2,1)} %cot_ref.1, bf16[96,768]{1,0:T(8,128)(2,1)} %bitcast.2, bf16[128,768]{1,0:T(8,128)(2,1)} %val_ref.1, bf16[128,768]{1,0:T(8,128)(2,1)} %gate_ref.1, ...), custom_call_target="tpu_custom_call" | custom-call | tf_op jit(solution)/shard_map/pallas_call | solution.py:428
  54.2 2.3 %shard_map.121 = (bf16[128,768]{1,0:T(8,128)(2,1)}, bf16[128,768]{1,0:T(8,128)(2,1)}, f32[128,768]{1,0:T(8,128)}, f32[96,768]{1,0:T(8,128)}) custom-call(bf16[768,128]{1,0:T(8,128)(2,1)} %get-tuple-element.12.gv_ref, bf16[128,768]{1,0:T(8,128)(2,1)} %get-tuple-element.13.gg_ref, bf16[768,128]{1,0:T(8,128)(2,1)} %get-tuple-element.14.gf_ref, ...), custom_call_target="tpu_custom_call" | custom-call | tf_op jit(solution)/shard_map/pallas_call | solution.py:471
